TPU v7x, 256 devices: a whole 4x4x8 slice. The times are simulated.
256 devices in a mesh: step: 32 (over z, x), seq: 8 (over y, core).
Axes of the slice: x: 4, y: 4, z: 8, core: 2. Of those that a mesh axis runs over, the one named last changes fastest.
Arguments:
- trajectory: bfloat16 [64, 1024, 2048], P('step', 'seq'), may hold values from -8 to 8
- initial: bfloat16 [1024, 2048], P('seq'), may hold values from -6 to 6
- step_sizes: float32 [64], P('step'), may hold values from 0.02 to 0.1
- time_index: int32 [64], P('step'), may hold values from 0 to 999, as said below
- plan: float32 [1000], replicated, may hold values from 0.02 to 80
- adaln_weight: bfloat16 [256, 4096], replicated, may hold values from -0.375 to 0.375
- query_weight: bfloat16 [2048, 1024], P('step'), may hold values from -1 to 1
- key_weight: bfloat16 [2048, 1024], P('step'), may hold values from -1 to 1
- value_weight: bfloat16 [2048, 1024], P('step'), may hold values from -0.125 to 0.125
- out_weight: bfloat16 [1024, 2048], P('step'), may hold values from -3 to 3
Outputs:
- updated: float32 [64, 1024, 2048], P('step', 'seq')
Inputs may be any that keep to these rules, and one draw needn't show every extreme that they name: `time_index`: strictly decreasing along the steps; the first is 999 and the last 0.
All inputs are finite; a program needn't handle non-finite values.
Results may differ from a plain program's by a relative error of at most 0.0054.
Values may be sent and summed in bfloat16 or wider, within the bound.
No kernel may reach another device: no remote copies, remote signals or barrier semaphores. Data moves between devices by JAX's collectives and lax.ppermute only.
A program may use at most 128 MiB of HBM per device.

v0:
```python
import functools

import jax
import jax.numpy as jnp
from jax import lax
from jax.experimental import pallas as pl
from jax.experimental.pallas import tpu as pltpu
from jax.sharding import PartitionSpec as P

HEAD_DIM = 64
EPS = 1e-06
BF16 = jnp.bfloat16
F32 = jnp.float32
MIB = 1024 * 1024
VMEM = pl.BlockSpec(memory_space=pltpu.VMEM)
SMEM = pl.BlockSpec(memory_space=pltpu.SMEM)
HBM = pl.BlockSpec(memory_space=pl.ANY)


def modulation(time_index, plan, adaln_weight):
    table_size = plan.shape[0]
    onehot = (time_index[:, None] == jnp.arange(table_size, dtype=jnp.int32)[None, :]).astype(F32)
    sigmas = jnp.sum(onehot * plan[None, :], axis=1)
    half_width = adaln_weight.shape[0] // 2
    frequency = 0.25 * jnp.exp(4.0 * jnp.arange(half_width, dtype=F32) / half_width)
    angles = jnp.log(sigmas)[:, None] * frequency[None, :]
    embedding = jnp.concatenate([jnp.cos(angles), jnp.sin(angles)], axis=1).astype(BF16)
    modulated = jnp.dot(embedding, adaln_weight, preferred_element_type=F32)
    feature_width = adaln_weight.shape[1] // 2
    return (modulated[:, :feature_width], modulated[:, feature_width:])


def pick_kernel(place_ref, query_ref, key_ref, value_ref, out_weight_ref, picked_ref):
    pair = picked_ref.shape[-1] // 4
    column = pl.multiple_of(place_ref[0] * pair, pair)
    blocks = [ref[:, pl.ds(column, pair)] for ref in (query_ref, key_ref, value_ref)]
    halves = []
    for half in range(2):
        start = pl.multiple_of((2 * place_ref[0] + half) * pair, pair)
        halves.append(out_weight_ref[:, pl.ds(start, pair)])
    picked = jnp.concatenate(blocks + [jnp.concatenate(halves, axis=0)], axis=1)
    for copy in range(picked_ref.shape[0]):
        picked_ref[copy] = picked


def pick(place, query_weight, key_weight, value_weight, out_weight, copies):
    rows = query_weight.shape[0]
    return pl.pallas_call(
        pick_kernel,
        out_shape=jax.ShapeDtypeStruct((copies, rows, 8 * HEAD_DIM), BF16),
        in_specs=[SMEM] + [VMEM] * 4,
        out_specs=VMEM,
        compiler_params=pltpu.CompilerParams(vmem_limit_bytes=60 * MIB),
        name="pick",
    )(place, query_weight, key_weight, value_weight, out_weight)


def normalize_kernel(shift_ref, gain_ref, rows_ref, out_ref):
    for step in range(2):
        floats = rows_ref[step].astype(F32)
        centered = floats - jnp.mean(floats, axis=-1, keepdims=True)
        variance = jnp.mean(centered * centered, axis=-1, keepdims=True)
        normed = centered * lax.rsqrt(variance + EPS)
        out_ref[step] = (normed * gain_ref[step : step + 1] + shift_ref[step : step + 1]).astype(
            BF16
        )


def normalize(shift, gain, rows):
    return pl.pallas_call(
        normalize_kernel,
        out_shape=jax.ShapeDtypeStruct(rows.shape, BF16),
        in_specs=[VMEM] * 3,
        out_specs=VMEM,
        compiler_params=pltpu.CompilerParams(vmem_limit_bytes=24 * MIB),
        cost_estimate=pl.CostEstimate(
            flops=16 * rows.size, bytes_accessed=8 * rows.size, transcendentals=0
        ),
        name="normalize",
    )(shift, gain, rows)


def tile_kernel(source_ref, tile_ref, half_ref, sems):
    pair = half_ref.shape[-1]
    across = half_ref.shape[0]
    start = source_ref.shape[-1] - pair
    loads = [
        pltpu.make_async_copy(
            source_ref.at[x, :, :, pl.ds(start, pair)], half_ref.at[x], sems.at[x]
        )
        for x in range(across)
    ]
    for load in loads:
        load.start()
    low = tile_ref.shape[2]
    for x, load in enumerate(loads):
        load.wait()
        for half in range(2):
            tile_ref[:, x, :, half * pair : (half + 1) * pair] = half_ref[
                x, :, half * low : (half + 1) * low
            ]


def tile_of(weights):
    across, depth, height, columns = weights.shape
    pair = columns // 4
    return pl.pallas_call(
        tile_kernel,
        out_shape=jax.ShapeDtypeStruct((depth, across, height // 2, 2 * pair), BF16),
        in_specs=[HBM],
        out_specs=VMEM,
        scratch_shapes=[
            pltpu.VMEM((across, depth, height, pair), BF16),
            pltpu.SemaphoreType.DMA((across,)),
        ],
        compiler_params=pltpu.CompilerParams(vmem_limit_bytes=60 * MIB),
        name="tile",
    )(weights).reshape(-1, 2 * pair)


def attend_kernel(place_ref, sizes_ref, source_ref, *refs):
    blocks, outs = refs[:10], refs[10:14]
    (
        sums_ref,
        parts_ref,
        keys_ref,
        values_ref,
        block_ref,
        order_ref,
        rows_ref,
        weight_ref,
        sems,
        weight_sems,
    ) = refs[14:]
    steps, groups, rows, width = rows_ref.shape
    pair = 2 * HEAD_DIM
    half = rows // 2

    fetches = [
        pltpu.make_async_copy(source_ref.at[x], weight_ref.at[:, x], weight_sems.at[x])
        for x in range(source_ref.shape[0])
    ]
    units = []
    for step in range(steps):
        for group in range(groups):
            pairs = []
            for side in range(2):
                if group < 3:
                    source = blocks[2 * group + side].at[step]
                else:
                    source = blocks[6 + 2 * side + step].at[0]
                pairs.append(
                    pltpu.make_async_copy(
                        source,
                        rows_ref.at[step, group, pl.ds(side * half, half)],
                        sems.at[step, group, side],
                    )
                )
            units.append(pairs)

    def start(unit):
        for load in units[unit] if unit < len(units) else []:
            load.start()

    for fetch in fetches:
        fetch.start()
    for unit in range(2):
        start(unit)
    values_ref[:, pair:] = jnp.ones((groups * rows, pair), BF16)
    for fetch in fetches:
        fetch.wait()
    for unit in range(2, 4):
        start(unit)

    weight = weight_ref.reshape(width, weight_ref.shape[-1])
    first = lax.broadcasted_iota(jnp.int32, (1, pair), 1) < HEAD_DIM
    scale = HEAD_DIM ** (-0.5)
    for step in range(steps):
        for group in range(groups):
            unit = step * groups + group
            for load in units[unit]:
                load.wait()
            start(unit + 4)
            part = jnp.dot(
                rows_ref[step, group], weight[:, : 3 * pair], preferred_element_type=F32
            ).astype(BF16)
            span = slice(group * rows, (group + 1) * rows)
            parts_ref[span, :] = part[:, :pair]
            keys_ref[span, :] = part[:, pair : 2 * pair]
            values_ref[span, :pair] = part[:, 2 * pair :]
        for position in range(groups):
            queries = parts_ref[position * rows : (position + 1) * rows, :].astype(F32) * scale
            heads = []
            for mask in (first, jnp.logical_not(first)):
                chosen = jnp.where(mask, queries, 0.0).astype(BF16)
                scores = lax.dot_general(
                    chosen, keys_ref[...], (((1,), (1,)), ((), ())), preferred_element_type=F32
                )
                weights = jnp.exp(scores - jnp.max(scores, axis=-1, keepdims=True)).astype(BF16)
                summed = jnp.dot(weights, values_ref[...], preferred_element_type=F32)
                heads.append(summed[:, :pair] / summed[:, pair:])
            attended = jnp.where(first, heads[0], heads[1]).astype(BF16)
            for side in range(2):
                block = attended[side * half : (side + 1) * half]
                spot = place_ref[2 * position + side]
                outs[position][side, step] = block
                scaled = sizes_ref[step] * block.astype(F32)
                if step == 0:
                    block_ref[spot] = scaled
                else:
                    block_ref[spot] = block_ref[spot] + scaled
    targets, depth = sums_ref.shape[:2]
    per = half // targets
    for field in range(block_ref.shape[0]):
        for turn in range(per):
            order_ref[pl.ds(per * field + turn, targets, stride=depth), :] = block_ref[
                field, turn * targets : (turn + 1) * targets
            ]
    sums_ref[...] = order_ref[...].astype(BF16).reshape(sums_ref.shape)


def attend(place, sizes, weights, blocks, targets):
    steps, half, width = blocks[0].shape
    across, depth, height, columns = weights.shape
    pair = columns // 4
    groups, rows = 4, 2 * half
    length = groups * rows
    block = jax.ShapeDtypeStruct((2, steps, half, pair), BF16)
    *outs, sums = pl.pallas_call(
        attend_kernel,
        out_shape=(block,) * groups
        + (jax.ShapeDtypeStruct((targets, length // targets, pair), BF16),),
        in_specs=[SMEM] * 2 + [HBM] * (1 + len(blocks)),
        out_specs=(VMEM,) * (groups + 1),
        scratch_shapes=[
            pltpu.VMEM((length, pair), BF16),
            pltpu.VMEM((length, pair), BF16),
            pltpu.VMEM((length, 2 * pair), BF16),
            pltpu.VMEM((2 * groups, half, pair), F32),
            pltpu.VMEM((length, pair), F32),
            pltpu.VMEM((steps, groups, rows, width), BF16),
            pltpu.VMEM((depth, across, height, columns), BF16),
            pltpu.SemaphoreType.DMA((steps, groups, 2)),
            pltpu.SemaphoreType.DMA((across,)),
        ],
        compiler_params=pltpu.CompilerParams(vmem_limit_bytes=60 * MIB),
        cost_estimate=pl.CostEstimate(
            flops=16 * length * length * pair + 12 * length * width * pair,
            bytes_accessed=4 * length * width + 8 * width * pair,
            transcendentals=4 * length * length,
        ),
        name="attend",
    )(place, sizes, weights, *blocks)
    return outs, sums


def earlier_kernel(sums_ref, out_ref):
    running = jnp.zeros(sums_ref.shape[1:], F32)
    for index in range(sums_ref.shape[0]):
        out_ref[index] = running.astype(BF16)
        running = running + sums_ref[index].astype(F32)


def earlier(sums):
    return pl.pallas_call(
        earlier_kernel,
        out_shape=jax.ShapeDtypeStruct(sums.shape, BF16),
        in_specs=[VMEM],
        out_specs=VMEM,
        compiler_params=pltpu.CompilerParams(vmem_limit_bytes=16 * MIB),
        name="earlier",
    )(sums)


def total_kernel(place_ref, heads_ref, sizes_ref, before_ref, initial_ref, *refs):
    blocks, tiles = refs[:8], refs[8:16]
    out_ref, order_ref, rows_ref, weight_ref, result_ref, load_sems, store_sems = refs[16:]
    groups, depth, pair = before_ref.shape
    rows = initial_ref.shape[0]
    per = rows // groups
    width = weight_ref.shape[-1]
    loads = [
        pltpu.make_async_copy(source, weight_ref.at[index], load_sems.at[index])
        for index, source in enumerate(tiles)
    ]
    for load in loads[:3]:
        load.start()

    order_ref[...] = before_ref[...].astype(F32).reshape(order_ref.shape)
    for field in range(depth // per):
        columns = slice(field * pair, (field + 1) * pair)
        for turn in range(per):
            rows_ref[turn * groups : (turn + 1) * groups, columns] = order_ref[
                pl.ds(per * field + turn, groups, stride=depth), :
            ].astype(BF16)
    for index, ref in enumerate(blocks):
        start = pl.multiple_of(heads_ref[index] * pair, pair)
        for step in range(2):
            rows_ref[(1 + step) * rows : (2 + step) * rows, pl.ds(start, pair)] = ref[
                index // 4, step
            ]

    stores = []
    for index, load in enumerate(loads):
        load.wait()
        for later in loads[index + 3 : index + 4]:
            later.start()
        start = pl.multiple_of(place_ref[index] * width, width)
        drift = jnp.dot(rows_ref[...], weight_ref[index], preferred_element_type=F32)
        base = (
            initial_ref[:, pl.ds(start, width)].astype(F32)
            + drift[:rows]
            + sizes_ref[0] * drift[rows : 2 * rows]
        )
        result_ref[index, 0] = base
        result_ref[index, 1] = base + sizes_ref[1] * drift[2 * rows :]
        store = pltpu.make_async_copy(
            result_ref.at[index], out_ref.at[:, :, pl.ds(start, width)], store_sems.at[index]
        )
        store.start()
        stores.append(store)
    for store in stores:
        store.wait()


def totals(place, heads, sizes, before, initial, blocks, tiles):
    rows, width = initial.shape
    groups, depth, pair = before.shape
    count = len(tiles)
    return pl.pallas_call(
        total_kernel,
        out_shape=jax.ShapeDtypeStruct((2, rows, width), F32),
        in_specs=[SMEM] * 3 + [VMEM] * 10 + [HBM] * 8,
        out_specs=HBM,
        scratch_shapes=[
            pltpu.VMEM((groups * depth, pair), F32),
            pltpu.VMEM((3 * rows, tiles[0].shape[0]), BF16),
            pltpu.VMEM((count,) + tiles[0].shape, BF16),
            pltpu.VMEM((count, 2, rows, tiles[0].shape[1]), F32),
            pltpu.SemaphoreType.DMA((count,)),
            pltpu.SemaphoreType.DMA((count,)),
        ],
        compiler_params=pltpu.CompilerParams(vmem_limit_bytes=60 * MIB),
        name="totals",
    )(place, heads, sizes, before, initial, *blocks, *tiles)


def gather_depth(blocks, shape):
    return lax.all_to_all(
        blocks,
        "step",
        0,
        0,
        axis_index_groups=[[x + shape[1] * z for z in range(shape[0])] for x in range(shape[1])],
    )


def gather_columns(block, shape):
    across = shape[1]
    return lax.all_to_all(
        jnp.broadcast_to(block[None], (across,) + block.shape),
        "step",
        0,
        0,
        axis_index_groups=[[z * across + x for x in range(across)] for z in range(shape[0])],
    )


def local(
    trajectory,
    initial,
    step_sizes,
    time_index,
    plan,
    adaln_weight,
    query_weight,
    key_weight,
    value_weight,
    out_weight,
):
    fields = lax.axis_size("seq")
    groups = lax.axis_size("step")
    chips = fields // 2
    shape = (groups // 4, 4)
    place = lax.axis_index("seq")
    chip, core = place // 2, place % 2
    pair = 2 * HEAD_DIM
    swap = [(i, i ^ 1) for i in range(fields)]

    def along_ring(block, by):
        return lax.ppermute(block, "seq", [(i, (i + 2 * by) % fields) for i in range(fields)])

    shifts_by = (1, chips - 1, 2)
    picked = pick(
        place[None].astype(jnp.int32),
        query_weight,
        key_weight,
        value_weight,
        out_weight,
        shape[0],
    )
    weights = gather_columns(gather_depth(picked, shape), shape)

    shifts, scales = modulation(time_index, plan, adaln_weight)
    gains = 1.0 + scales

    source_chips = [chip] + [(chip - by) % chips for by in shifts_by]
    places = jnp.stack(
        [spot for source in source_chips for spot in (2 * source + core, 2 * source + 1 - core)]
    ).astype(jnp.int32)

    def partner_of(block):
        return lax.ppermute(block, "seq", swap)

    here = normalize(shifts, gains, trajectory)
    behind, ahead = along_ring(here, 1), along_ring(here, chips - 1)
    opposite = [along_ring(behind[:1], 1), along_ring(ahead[1:], chips - 1)]
    blocks = []
    for block in (here, behind, ahead):
        blocks += [block, partner_of(block)]
    blocks += opposite + [partner_of(block) for block in opposite]
    out_tile = tile_of(weights)
    out_tiles = [out_tile] + [along_ring(out_tile, by) for by in shifts_by]
    attended, sums = attend(places, step_sizes, weights, blocks, groups)
    out_tiles, _ = lax.optimization_barrier((out_tiles, sums))
    out_tiles = out_tiles + [partner_of(tile) for tile in out_tiles]

    per = sums.shape[1] // fields
    received = lax.all_to_all(
        sums.reshape(groups * fields, per, pair), ("step", "seq"), 0, 0
    ).reshape(sums.shape)
    before = lax.all_to_all(earlier(received), "step", 0, 0)

    arrived = [attended[0]] + [
        along_ring(block, chips - by) for block, by in zip(attended[1:], shifts_by)
    ]
    arrived = arrived + [partner_of(block) for block in arrived]
    sources = [chip] + [(chip + by) % chips for by in shifts_by]
    heads = jnp.stack(
        [2 * source + core for source in sources] + [2 * source + 1 - core for source in sources]
    ).astype(jnp.int32)
    spots = jnp.concatenate([places[0::2], places[1::2]])
    return totals(spots, heads, step_sizes, before, initial, arrived, out_tiles)


def solution(mesh):
    in_specs = (
        P("step", "seq", None),
        P("seq", None),
        P("step"),
        P("step"),
        P(),
        P(),
        P("step", None),
        P("step", None),
        P("step", None),
        P("step", None),
    )
    out_specs = P("step", "seq", None)
    return jax.shard_map(local, mesh=mesh, in_specs=in_specs, out_specs=out_specs, check_vma=False)
```

profile of v0, /device:TPU:1, one launch (start us, length us, event | category | flops | bytes accessed | tf_op | source)
XLA Modules:
  0.0 140.3 jit_solution(13658123292058626537)
XLA Ops:
  0.0 2.1 %pick.1 = bf16[8,64,512]{2,1,0:T(8,128)(2,1)} custom-call(s32[1]{0:T(128)} %bitcast.14.place_ref, bf16[64,1024]{1,0:T(8,128)(2,1)} %query_ref.1, bf16[64,1024]{1,0:T(8,128)(2,1)} %key_ref.1, bf16[64,1024]{1,0:T(8,128)(2,1)} %value_ref.1, bf16[32,2048]{1,0:T(8,128)(2,1)} %out_weight_ref.1), custom_call_target="tpu_custom_call" | custom-call | tf_op jit(solution)/shard_map/pick/pallas_call | solution.py:48
  2.1 9.0 %all-to-all-start = ((bf16[8,64,512]{2,1,0:T(8,128)(2,1)}), bf16[8,64,512]{2,1,0:T(8,128)(2,1)}, u32[]{:S(2)}, u32[]{:S(2)}) async-start(bf16[8,64,512]{2,1,0:T(8,128)(2,1)} %pick.1), calls=%async_computation | async-start | bytes 1048576 | tf_op jit(solution)/shard_map/all_to_all | solution.py:349
  11.1 0.2 fusion
  11.3 0.1 fusion.1
  11.5 0.4 fusion.3
  11.9 1.7 %normalize.1.refs_0_ = bf16[2,128,2048]{2,1,0:T(8,128)(2,1)} custom-call(f32[2,2048]{1,0:T(2,128)S(1)} %get-tuple-element.24.shift_ref, f32[2,2048]{1,0:T(2,128)S(1)} %get-tuple-element.23.gain_ref, bf16[2,128,2048]{2,1,0:T(8,128)(2,1)S(1)} %copy-done.1), custom_call_target="tpu_custom_call" | custom-call | flops 8388608 | bytes 4194304 | tf_op jit(solution)/shard_map/normalize/pallas_call | solution.py:70
  13.6 1.3 collective-permute-start.1
  14.9 1.4 %collective-permute-start.3 = (bf16[2,128,2048]{2,1,0:T(8,128)(2,1)}, bf16[2,128,2048]{2,1,0:T(8,128)(2,1)}, u32[]{:S(2)}, u32[]{:S(2)}) collective-permute-start(bf16[2,128,2048]{2,1,0:T(8,128)(2,1)} %normalize.1.refs_0_), channel_id=1, source_target_pairs={{0,6},{1,7},{2,0},{3,1},{4,2},{5,3},{6,4},{7,5},{8,14},{9,15},{10,... | collective-permute-start | bytes 3145736 | tf_op jit(solution)/shard_map/ppermute | solution.py:391
  16.4 12.8 %all-to-all-done = bf16[8,64,512]{2,1,0:T(8,128)(2,1)} async-done(((bf16[8,64,512]{2,1,0:T(8,128)(2,1)}), bf16[8,64,512]{2,1,0:T(8,128)(2,1)}, u32[]{:S(2)}, u32[]{:S(2)}) %all-to-all-start) | async-done | bytes 524320 | tf_op jit(solution)/shard_map/all_to_all | solution.py:349
  29.2 2.6 %broadcast_in_dim.5 = bf16[4,8,64,512]{3,2,1,0:T(8,128)(2,1)} broadcast(bf16[8,64,512]{2,1,0:T(8,128)(2,1)} %all-to-all-done), dimensions={1,2,3} | broadcast | bytes 2621440 | tf_op jit(solution)/shard_map/broadcast_in_dim | solution.py:361
  31.8 4.5 %all-to-all-start.1 = ((bf16[4,8,64,512]{3,2,1,0:T(8,128)(2,1)}), bf16[4,8,64,512]{3,2,1,0:T(8,128)(2,1)}, u32[]{:S(2)}, u32[]{:S(2)}) async-start(bf16[4,8,64,512]{3,2,1,0:T(8,128)(2,1)} %broadcast_in_dim.5), calls=%async_computation.1 | async-start | bytes 4194304 | tf_op jit(solution)/shard_map/all_to_all | solution.py:360
  36.2 0.6 collective-permute-start
  36.8 2.2 %collective-permute-done.1.refs_2_ = bf16[2,128,2048]{2,1,0:T(8,128)(2,1)} collective-permute-done((bf16[2,128,2048]{2,1,0:T(8,128)(2,1)}, bf16[2,128,2048]{2,1,0:T(8,128)(2,1)}, u32[]{:S(2)}, u32[]{:S(2)}) %collective-permute-start.1) | collective-permute-done | bytes 1048608 | tf_op jit(solution)/shard_map/ppermute | solution.py:391
  39.0 1.1 slice.26
  40.1 0.1 collective-permute-start.5
  40.2 2.1 %collective-permute-start.2 = (bf16[2,128,2048]{2,1,0:T(8,128)(2,1)}, bf16[2,128,2048]{2,1,0:T(8,128)(2,1)}, u32[]{:S(2)}, u32[]{:S(2)}) collective-permute-start(bf16[2,128,2048]{2,1,0:T(8,128)(2,1)} %collective-permute-done.1.refs_2_), channel_id=1, source_target_pairs={{0,1},{1,0},{2,3},{3,2},{4,5},{5,4},{6,7},{7,6},{8,9},{9,8},{10,11... | collective-permute-start | bytes 3145736 | tf_op jit(solution)/shard_map/ppermute | solution.py:413
  42.3 0.0 collective-permute-start.4
  42.3 1.1 slice.27
  43.3 2.7 %collective-permute-start.6 = (bf16[1,128,2048]{2,1,0:T(8,128)(2,1)S(1)}, bf16[1,128,2048]{2,1,0:T(8,128)(2,1)}, u32[]{:S(2)}, u32[]{:S(2)}) collective-permute-start(bf16[1,128,2048]{2,1,0:T(8,128)(2,1)S(1)} %slice.27), channel_id=1, source_target_pairs={{0,6},{1,7},{2,0},{3,1},{4,2},{5,3},{6,4},{7,5},{8,14},{9,15},{10,... | collective-permute-start | bytes 1572872 | tf_op jit(solution)/shard_map/ppermute | solution.py:391
  46.1 7.0 %collective-permute-done.5.refs_6_ = bf16[1,128,2048]{2,1,0:T(8,128)(2,1)} collective-permute-done((bf16[1,128,2048]{2,1,0:T(8,128)(2,1)S(1)}, bf16[1,128,2048]{2,1,0:T(8,128)(2,1)}, u32[]{:S(2)}, u32[]{:S(2)}) %collective-permute-start.5) | collective-permute-done | bytes 524320 | tf_op jit(solution)/shard_map/ppermute | solution.py:391
  53.1 2.7 %collective-permute-start.7 = (bf16[1,128,2048]{2,1,0:T(8,128)(2,1)}, bf16[1,128,2048]{2,1,0:T(8,128)(2,1)}, u32[]{:S(2)}, u32[]{:S(2)}) collective-permute-start(bf16[1,128,2048]{2,1,0:T(8,128)(2,1)} %collective-permute-done.5.refs_6_), channel_id=1, source_target_pairs={{0,1},{1,0},{2,3},{3,2},{4,5},{5,4},{6,7},{7,6},{8,9},{9,8},{10,11... | collective-permute-start | bytes 1572872 | tf_op jit(solution)/shard_map/ppermute | solution.py:413
  55.8 1.0 collective-permute-done.6.refs_7_
  56.8 1.4 collective-permute-start.8
  58.2 0.7 stack.58.place_ref
  58.9 3.4 %all-to-all-done.1.source_ref = bf16[4,8,64,512]{3,2,1,0:T(8,128)(2,1)} async-done(((bf16[4,8,64,512]{3,2,1,0:T(8,128)(2,1)}), bf16[4,8,64,512]{3,2,1,0:T(8,128)(2,1)}, u32[]{:S(2)}, u32[]{:S(2)}) %all-to-all-start.1) | async-done | bytes 2097184 | tf_op jit(solution)/shard_map/all_to_all | solution.py:360
  62.2 2.0 %tile.1 = bf16[8,4,32,256]{3,2,1,0:T(8,128)(2,1)} custom-call(bf16[4,8,64,512]{3,2,1,0:T(8,128)(2,1)} %all-to-all-done.1.source_ref), custom_call_target="tpu_custom_call" | custom-call | tf_op jit(solution)/shard_map/tile/pallas_call | solution.py:107
  64.3 0.0 collective-permute-done.refs_1_
  64.3 0.0 copy-start.12
  64.3 1.0 copy-done.12
  65.2 1.3 collective-permute-start.16
  66.5 1.5 %collective-permute-start.17 = (bf16[1024,256]{1,0:T(8,128)(2,1)}, bf16[1024,256]{1,0:T(8,128)(2,1)}, u32[]{:S(2)}, u32[]{:S(2)}) collective-permute-start(bf16[1024,256]{1,0:T(8,128)(2,1)} %bitcast.21), channel_id=1, source_target_pairs={{0,6},{1,7},{2,0},{3,1},{4,2},{5,3},{6,4},{7,5},{8,14},{9,15},{10,... | collective-permute-start | bytes 1572872 | tf_op jit(solution)/shard_map/ppermute | solution.py:391
  68.1 1.6 %collective-permute-start.18 = (bf16[1024,256]{1,0:T(8,128)(2,1)}, bf16[1024,256]{1,0:T(8,128)(2,1)}, u32[]{:S(2)}, u32[]{:S(2)}) collective-permute-start(bf16[1024,256]{1,0:T(8,128)(2,1)} %bitcast.22), channel_id=1, source_target_pairs={{0,4},{1,5},{2,6},{3,7},{4,0},{5,1},{6,2},{7,3},{8,12},{9,13},{10,... | collective-permute-start | bytes 1572872 | tf_op jit(solution)/shard_map/ppermute | solution.py:391
  69.6 15.2 %attend.1 = (bf16[2,2,128,128]{3,2,1,0:T(8,128)(2,1)}, bf16[2,2,128,128]{3,2,1,0:T(8,128)(2,1)}, bf16[2,2,128,128]{3,2,1,0:T(8,128)(2,1)}, bf16[2,2,128,128]{3,2,1,0:T(8,128)(2,1)}, bf16[32,32,128]{2,1,0:T(8,128)(2,1)}) custom-call(s32[8]{0:T(128)} %stack.58.place_ref, f32[2]{0:T(128)} %sizes_ref.3, bf16[4,8,64,512]{3,2,1,0:T(8,128)(2,1)} %all-to-all-done.1.source_ref, ...), custom_call_target="tpu_custom_call" | custom-call | flops 5368709120 | bytes 10485760 | tf_op jit(solution)/shard_map/attend/pallas_call | solution.py:229
  84.8 9.1 %all-to-all-start.2 = ((bf16[256,4,128]{2,1,0:T(4,128)(2,1)}), bf16[256,4,128]{2,1,0:T(4,128)(2,1)S(1)}, u32[]{:S(2)}, u32[]{:S(2)}) async-start(bf16[256,4,128]{2,1,0:T(4,128)(2,1)} %bitcast.25), calls=%async_computation.2 | async-start | bytes 524288 | tf_op jit(solution)/shard_map/all_to_all | solution.py:429
  93.9 2.7 %collective-permute-start.9 = (bf16[2,2,128,128]{3,2,1,0:T(8,128)(2,1)}, bf16[2,2,128,128]{3,2,1,0:T(8,128)(2,1)S(1)}, u32[]{:S(2)}, u32[]{:S(2)}) collective-permute-start(bf16[2,2,128,128]{3,2,1,0:T(8,128)(2,1)} %get-tuple-element.16), channel_id=1, source_target_pairs={{0,6},{1,7},{2,0},{3,1},{4,2},{5,3},{6,4},{7,5},{8,14},{9,15},{10,... | collective-permute-start | bytes 393224 | tf_op jit(solution)/shard_map/ppermute | solution.py:391
  96.7 0.0 collective-permute-start.10
  96.7 0.0 collective-permute-done.16.refs_9_
  96.7 1.7 %collective-permute-start.11 = (bf16[2,2,128,128]{3,2,1,0:T(8,128)(2,1)}, bf16[2,2,128,128]{3,2,1,0:T(8,128)(2,1)S(1)}, u32[]{:S(2)}, u32[]{:S(2)}) collective-permute-start(bf16[2,2,128,128]{3,2,1,0:T(8,128)(2,1)} %get-tuple-element.18), channel_id=1, source_target_pairs={{0,4},{1,5},{2,6},{3,7},{4,0},{5,1},{6,2},{7,3},{8,12},{9,13},{10,... | collective-permute-start | bytes 393224 | tf_op jit(solution)/shard_map/ppermute | solution.py:391
  98.4 0.0 collective-permute-done.17.refs_10_
  98.4 1.2 collective-permute-start.12
  99.6 0.0 collective-permute-done.18.refs_11_
  99.6 0.1 collective-permute-start.19
  99.7 0.6 collective-permute-done.9.refs_1_
  100.3 5.4 %collective-permute-start.20 = (bf16[1024,256]{1,0:T(8,128)(2,1)S(1)}, bf16[1024,256]{1,0:T(8,128)(2,1)}, u32[]{:S(2)}, u32[]{:S(2)}) collective-permute-start(bf16[1024,256]{1,0:T(8,128)(2,1)S(1)} %collective-permute-done.16.refs_9_), channel_id=1, source_target_pairs={{0,1},{1,0},{2,3},{3,2},{4,5},{5,4},{6,7},{7,6},{8,9},{9,8},{10,11... | collective-permute-start | bytes 1572872 | tf_op jit(solution)/shard_map/ppermute | solution.py:413
  105.6 3.2 %collective-permute-start.21 = (bf16[1024,256]{1,0:T(8,128)(2,1)}, bf16[1024,256]{1,0:T(8,128)(2,1)}, u32[]{:S(2)}, u32[]{:S(2)}) collective-permute-start(bf16[1024,256]{1,0:T(8,128)(2,1)} %collective-permute-done.17.refs_10_), channel_id=1, source_target_pairs={{0,1},{1,0},{2,3},{3,2},{4,5},{5,4},{6,7},{7,6},{8,9},{9,8},{10,11... | collective-permute-start | bytes 1572872 | tf_op jit(solution)/shard_map/ppermute | solution.py:413
  108.8 0.0 collective-permute-done.11.refs_3_
  108.9 0.7 copy-done.7
  109.5 0.6 collective-permute-start.22
  110.2 0.7 earlier.1
  110.9 8.6 %all-to-all-start.3 = ((bf16[32,32,128]{2,1,0:T(8,128)(2,1)}), bf16[32,32,128]{2,1,0:T(8,128)(2,1)S(1)}, u32[]{:S(2)}, u32[]{:S(2)}) async-start(bf16[32,32,128]{2,1,0:T(8,128)(2,1)} %earlier.1), calls=%async_computation.3 | async-start | bytes 524288 | tf_op jit(solution)/shard_map/all_to_all | solution.py:432
  119.5 0.4 collective-permute-start.13
  119.9 1.1 collective-permute-done.13.refs_5_
  121.0 0.6 copy-done.8
  121.6 0.3 collective-permute-start.14
  121.9 1.4 %collective-permute-done.14.refs_6_ = bf16[2,2,128,128]{3,2,1,0:T(8,128)(2,1)} collective-permute-done((bf16[2,2,128,128]{3,2,1,0:T(8,128)(2,1)}, bf16[2,2,128,128]{3,2,1,0:T(8,128)(2,1)}, u32[]{:S(2)}, u32[]{:S(2)}) %collective-permute-start.14) | collective-permute-done | bytes 131104 | tf_op jit(solution)/shard_map/ppermute | solution.py:413
  123.3 0.3 collective-permute-start.15
  123.6 0.1 slice.19
  123.7 0.1 slice.18
  123.8 0.6 stack.65.heads_ref
  124.4 0.6 pad_add_fusion.place_ref
  125.0 0.0 collective-permute-done.15.refs_7_
  125.0 6.5 %all-to-all-done.3.before_ref = bf16[32,32,128]{2,1,0:T(8,128)(2,1)S(1)} async-done(((bf16[32,32,128]{2,1,0:T(8,128)(2,1)}), bf16[32,32,128]{2,1,0:T(8,128)(2,1)S(1)}, u32[]{:S(2)}, u32[]{:S(2)}) %all-to-all-start.3) | async-done | bytes 262176 | tf_op jit(solution)/shard_map/all_to_all | solution.py:432
  131.6 0.7 copy-done.3
  132.2 7.8 %totals.1 = f32[2,128,2048]{2,1,0:T(8,128)} custom-call(s32[8]{0:T(128)} %pad_add_fusion.place_ref, s32[8]{0:T(128)} %stack.65.heads_ref, f32[2]{0:T(128)} %sizes_ref.3, bf16[32,32,128]{2,1,0:T(8,128)(2,1)} %copy-done.3, bf16[128,2048]{1,0:T(8,128)(2,1)} %initial_ref.1, bf16[2,2,128,128]{3,2,1,0:T(8,128)(2,1)} %get-tuple-element.15.refs_0_, ...), custom_call_target="tpu_custom_call" | custom-call | tf_op jit(solution)/shard_map/totals/pallas_call | solution.py:330
  (36 shorter events, 0.1 us)
Async XLA Ops:
  0.0 11.5 %copy-start = (bf16[256,4096]{1,0:T(8,128)(2,1)S(1)}, bf16[256,4096]{1,0:T(8,128)(2,1)}, u32[]{:S(2)}) copy-start(bf16[256,4096]{1,0:T(8,128)(2,1)} %param.15) | copy-start | bytes 6291460
  0.0 11.1 %copy-start.10 = (s32[2]{0:T(128)S(1)}, s32[2]{0:T(128)}, u32[]{:S(2)}) copy-start(s32[2]{0:T(128)} %param.13) | copy-start | bytes 28
  0.0 11.1 %copy-start.9 = (f32[1000]{0:T(1024)S(1)}, f32[1000]{0:T(1024)}, u32[]{:S(2)}) copy-start(f32[1000]{0:T(1024)} %param.14) | copy-start | bytes 12004
  0.0 11.9 %copy-start.1 = (bf16[2,128,2048]{2,1,0:T(8,128)(2,1)S(1)}, bf16[2,128,2048]{2,1,0:T(8,128)(2,1)}, u32[]{:S(2)}) copy-start(bf16[2,128,2048]{2,1,0:T(8,128)(2,1)} %rows_ref.1) | copy-start | bytes 3145732
  2.1 27.1 %all-to-all-start = ((bf16[8,64,512]{2,1,0:T(8,128)(2,1)}), bf16[8,64,512]{2,1,0:T(8,128)(2,1)}, u32[]{:S(2)}, u32[]{:S(2)}) async-start(bf16[8,64,512]{2,1,0:T(8,128)(2,1)} %pick.1), calls=%async_computation | async-start | bytes 1048576 | tf_op jit(solution)/shard_map/all_to_all | solution.py:349
  13.6 25.4 %collective-permute-start.1 = (bf16[2,128,2048]{2,1,0:T(8,128)(2,1)}, bf16[2,128,2048]{2,1,0:T(8,128)(2,1)}, u32[]{:S(2)}, u32[]{:S(2)}) collective-permute-start(bf16[2,128,2048]{2,1,0:T(8,128)(2,1)} %normalize.1.refs_0_), channel_id=1, source_target_pairs={{0,2},{1,3},{2,4},{3,5},{4,6},{5,7},{6,0},{7,1},{8,10},{9,11},{10,... | collective-permute-start | bytes 3145736 | tf_op jit(solution)/shard_map/ppermute | solution.py:391
  14.9 27.3 %collective-permute-start.3 = (bf16[2,128,2048]{2,1,0:T(8,128)(2,1)}, bf16[2,128,2048]{2,1,0:T(8,128)(2,1)}, u32[]{:S(2)}, u32[]{:S(2)}) collective-permute-start(bf16[2,128,2048]{2,1,0:T(8,128)(2,1)} %normalize.1.refs_0_), channel_id=1, source_target_pairs={{0,6},{1,7},{2,0},{3,1},{4,2},{5,3},{6,4},{7,5},{8,14},{9,15},{10,... | collective-permute-start | bytes 3145736 | tf_op jit(solution)/shard_map/ppermute | solution.py:391
  31.8 30.5 %all-to-all-start.1 = ((bf16[4,8,64,512]{3,2,1,0:T(8,128)(2,1)}), bf16[4,8,64,512]{3,2,1,0:T(8,128)(2,1)}, u32[]{:S(2)}, u32[]{:S(2)}) async-start(bf16[4,8,64,512]{3,2,1,0:T(8,128)(2,1)} %broadcast_in_dim.5), calls=%async_computation.1 | async-start | bytes 4194304 | tf_op jit(solution)/shard_map/all_to_all | solution.py:360
  36.2 28.0 %collective-permute-start = (bf16[2,128,2048]{2,1,0:T(8,128)(2,1)}, bf16[2,128,2048]{2,1,0:T(8,128)(2,1)S(1)}, u32[]{:S(2)}, u32[]{:S(2)}) collective-permute-start(bf16[2,128,2048]{2,1,0:T(8,128)(2,1)} %normalize.1.refs_0_), channel_id=1, source_target_pairs={{0,1},{1,0},{2,3},{3,2},{4,5},{5,4},{6,7},{7,6},{8,9},{9,8},{10,11... | collective-permute-start | bytes 3145736 | tf_op jit(solution)/shard_map/ppermute | solution.py:413
  40.1 13.0 %collective-permute-start.5 = (bf16[1,128,2048]{2,1,0:T(8,128)(2,1)S(1)}, bf16[1,128,2048]{2,1,0:T(8,128)(2,1)}, u32[]{:S(2)}, u32[]{:S(2)}) collective-permute-start(bf16[1,128,2048]{2,1,0:T(8,128)(2,1)S(1)} %slice.26), channel_id=1, source_target_pairs={{0,2},{1,3},{2,4},{3,5},{4,6},{5,7},{6,0},{7,1},{8,10},{9,11},{10,... | collective-permute-start | bytes 1572872 | tf_op jit(solution)/shard_map/ppermute | solution.py:391
  40.2 26.4 %collective-permute-start.2 = (bf16[2,128,2048]{2,1,0:T(8,128)(2,1)}, bf16[2,128,2048]{2,1,0:T(8,128)(2,1)}, u32[]{:S(2)}, u32[]{:S(2)}) collective-permute-start(bf16[2,128,2048]{2,1,0:T(8,128)(2,1)} %collective-permute-done.1.refs_2_), channel_id=1, source_target_pairs={{0,1},{1,0},{2,3},{3,2},{4,5},{5,4},{6,7},{7,6},{8,9},{9,8},{10,11... | collective-permute-start | bytes 3145736 | tf_op jit(solution)/shard_map/ppermute | solution.py:413
  42.3 25.8 %collective-permute-start.4 = (bf16[2,128,2048]{2,1,0:T(8,128)(2,1)}, bf16[2,128,2048]{2,1,0:T(8,128)(2,1)}, u32[]{:S(2)}, u32[]{:S(2)}) collective-permute-start(bf16[2,128,2048]{2,1,0:T(8,128)(2,1)} %collective-permute-done.3.refs_4_), channel_id=1, source_target_pairs={{0,1},{1,0},{2,3},{3,2},{4,5},{5,4},{6,7},{7,6},{8,9},{9,8},{10,11... | collective-permute-start | bytes 3145736 | tf_op jit(solution)/shard_map/ppermute | solution.py:413
  43.3 13.5 %collective-permute-start.6 = (bf16[1,128,2048]{2,1,0:T(8,128)(2,1)S(1)}, bf16[1,128,2048]{2,1,0:T(8,128)(2,1)}, u32[]{:S(2)}, u32[]{:S(2)}) collective-permute-start(bf16[1,128,2048]{2,1,0:T(8,128)(2,1)S(1)} %slice.27), channel_id=1, source_target_pairs={{0,6},{1,7},{2,0},{3,1},{4,2},{5,3},{6,4},{7,5},{8,14},{9,15},{10,... | collective-permute-start | bytes 1572872 | tf_op jit(solution)/shard_map/ppermute | solution.py:391
  53.1 16.6 %collective-permute-start.7 = (bf16[1,128,2048]{2,1,0:T(8,128)(2,1)}, bf16[1,128,2048]{2,1,0:T(8,128)(2,1)}, u32[]{:S(2)}, u32[]{:S(2)}) collective-permute-start(bf16[1,128,2048]{2,1,0:T(8,128)(2,1)} %collective-permute-done.5.refs_6_), channel_id=1, source_target_pairs={{0,1},{1,0},{2,3},{3,2},{4,5},{5,4},{6,7},{7,6},{8,9},{9,8},{10,11... | collective-permute-start | bytes 1572872 | tf_op jit(solution)/shard_map/ppermute | solution.py:413
  56.8 12.8 %collective-permute-start.8 = (bf16[1,128,2048]{2,1,0:T(8,128)(2,1)}, bf16[1,128,2048]{2,1,0:T(8,128)(2,1)}, u32[]{:S(2)}, u32[]{:S(2)}) collective-permute-start(bf16[1,128,2048]{2,1,0:T(8,128)(2,1)} %collective-permute-done.6.refs_7_), channel_id=1, source_target_pairs={{0,1},{1,0},{2,3},{3,2},{4,5},{5,4},{6,7},{7,6},{8,9},{9,8},{10,11... | collective-permute-start | bytes 1572872 | tf_op jit(solution)/shard_map/ppermute | solution.py:413
  64.3 1.0 copy-start.12
  65.2 34.3 %copy-start.2 = (bf16[8,4,32,256]{3,2,1,0:T(8,128)(2,1)S(1)}, bf16[8,4,32,256]{3,2,1,0:T(8,128)(2,1)}, u32[]{:S(2)}) copy-start(bf16[8,4,32,256]{3,2,1,0:T(8,128)(2,1)} %tile.1) | copy-start | bytes 1572868
  65.2 58.4 %copy-start.11 = (s32[8]{0:T(128)S(1)}, s32[8]{0:T(128)}, u32[]{:S(2)}) copy-start(s32[8]{0:T(128)} %stack.58.place_ref) | copy-start | bytes 100
  65.2 31.4 %collective-permute-start.16 = (bf16[1024,256]{1,0:T(8,128)(2,1)}, bf16[1024,256]{1,0:T(8,128)(2,1)S(1)}, u32[]{:S(2)}, u32[]{:S(2)}) collective-permute-start(bf16[1024,256]{1,0:T(8,128)(2,1)} %bitcast.20), channel_id=1, source_target_pairs={{0,2},{1,3},{2,4},{3,5},{4,6},{5,7},{6,0},{7,1},{8,10},{9,11},{10,... | collective-permute-start | bytes 1572872 | tf_op jit(solution)/shard_map/ppermute | solution.py:391
  66.5 31.8 %collective-permute-start.17 = (bf16[1024,256]{1,0:T(8,128)(2,1)}, bf16[1024,256]{1,0:T(8,128)(2,1)}, u32[]{:S(2)}, u32[]{:S(2)}) collective-permute-start(bf16[1024,256]{1,0:T(8,128)(2,1)} %bitcast.21), channel_id=1, source_target_pairs={{0,6},{1,7},{2,0},{3,1},{4,2},{5,3},{6,4},{7,5},{8,14},{9,15},{10,... | collective-permute-start | bytes 1572872 | tf_op jit(solution)/shard_map/ppermute | solution.py:391
  68.1 31.5 %collective-permute-start.18 = (bf16[1024,256]{1,0:T(8,128)(2,1)}, bf16[1024,256]{1,0:T(8,128)(2,1)}, u32[]{:S(2)}, u32[]{:S(2)}) collective-permute-start(bf16[1024,256]{1,0:T(8,128)(2,1)} %bitcast.22), channel_id=1, source_target_pairs={{0,4},{1,5},{2,6},{3,7},{4,0},{5,1},{6,2},{7,3},{8,12},{9,13},{10,... | collective-permute-start | bytes 1572872 | tf_op jit(solution)/shard_map/ppermute | solution.py:391
  84.8 25.3 %all-to-all-start.2 = ((bf16[256,4,128]{2,1,0:T(4,128)(2,1)}), bf16[256,4,128]{2,1,0:T(4,128)(2,1)S(1)}, u32[]{:S(2)}, u32[]{:S(2)}) async-start(bf16[256,4,128]{2,1,0:T(4,128)(2,1)} %bitcast.25), calls=%async_computation.2 | async-start | bytes 524288 | tf_op jit(solution)/shard_map/all_to_all | solution.py:429
  93.9 6.3 %collective-permute-start.9 = (bf16[2,2,128,128]{3,2,1,0:T(8,128)(2,1)}, bf16[2,2,128,128]{3,2,1,0:T(8,128)(2,1)S(1)}, u32[]{:S(2)}, u32[]{:S(2)}) collective-permute-start(bf16[2,2,128,128]{3,2,1,0:T(8,128)(2,1)} %get-tuple-element.16), channel_id=1, source_target_pairs={{0,6},{1,7},{2,0},{3,1},{4,2},{5,3},{6,4},{7,5},{8,14},{9,15},{10,... | collective-permute-start | bytes 393224 | tf_op jit(solution)/shard_map/ppermute | solution.py:391
  96.7 9.0 %collective-permute-start.10 = (bf16[2,2,128,128]{3,2,1,0:T(8,128)(2,1)}, bf16[2,2,128,128]{3,2,1,0:T(8,128)(2,1)S(1)}, u32[]{:S(2)}, u32[]{:S(2)}) collective-permute-start(bf16[2,2,128,128]{3,2,1,0:T(8,128)(2,1)} %get-tuple-element.17), channel_id=1, source_target_pairs={{0,2},{1,3},{2,4},{3,5},{4,6},{5,7},{6,0},{7,1},{8,10},{9,11},{10,... | collective-permute-start | bytes 393224 | tf_op jit(solution)/shard_map/ppermute | solution.py:391
  96.7 34.9 %copy-start.4 = (bf16[1024,256]{1,0:T(8,128)(2,1)}, bf16[1024,256]{1,0:T(8,128)(2,1)S(1)}, u32[]{:S(2)}) copy-start(bf16[1024,256]{1,0:T(8,128)(2,1)S(1)} %collective-permute-done.16.refs_9_) | copy-start | bytes 1572868
  96.7 12.2 %collective-permute-start.11 = (bf16[2,2,128,128]{3,2,1,0:T(8,128)(2,1)}, bf16[2,2,128,128]{3,2,1,0:T(8,128)(2,1)S(1)}, u32[]{:S(2)}, u32[]{:S(2)}) collective-permute-start(bf16[2,2,128,128]{3,2,1,0:T(8,128)(2,1)} %get-tuple-element.18), channel_id=1, source_target_pairs={{0,4},{1,5},{2,6},{3,7},{4,0},{5,1},{6,2},{7,3},{8,12},{9,13},{10,... | collective-permute-start | bytes 393224 | tf_op jit(solution)/shard_map/ppermute | solution.py:391
  98.4 21.2 %collective-permute-start.12 = (bf16[2,2,128,128]{3,2,1,0:T(8,128)(2,1)}, bf16[2,2,128,128]{3,2,1,0:T(8,128)(2,1)}, u32[]{:S(2)}, u32[]{:S(2)}) collective-permute-start(bf16[2,2,128,128]{3,2,1,0:T(8,128)(2,1)} %get-tuple-element.15.refs_0_), channel_id=1, source_target_pairs={{0,1},{1,0},{2,3},{3,2},{4,5},{5,4},{6,7},{7,6},{8,9},{9,8},{10,11... | collective-permute-start | bytes 393224 | tf_op jit(solution)/shard_map/ppermute | solution.py:413
  99.6 32.0 %collective-permute-start.19 = (bf16[1024,256]{1,0:T(8,128)(2,1)S(1)}, bf16[1024,256]{1,0:T(8,128)(2,1)}, u32[]{:S(2)}, u32[]{:S(2)}) collective-permute-start(bf16[1024,256]{1,0:T(8,128)(2,1)S(1)} %bitcast.24), channel_id=1, source_target_pairs={{0,1},{1,0},{2,3},{3,2},{4,5},{5,4},{6,7},{7,6},{8,9},{9,8},{10,11... | collective-permute-start | bytes 1572872 | tf_op jit(solution)/shard_map/ppermute | solution.py:413
  100.3 31.3 %copy-start.5 = (bf16[2,2,128,128]{3,2,1,0:T(8,128)(2,1)}, bf16[2,2,128,128]{3,2,1,0:T(8,128)(2,1)S(1)}, u32[]{:S(2)}) copy-start(bf16[2,2,128,128]{3,2,1,0:T(8,128)(2,1)S(1)} %collective-permute-done.9.refs_1_) | copy-start | bytes 393220
  100.3 31.3 %collective-permute-start.20 = (bf16[1024,256]{1,0:T(8,128)(2,1)S(1)}, bf16[1024,256]{1,0:T(8,128)(2,1)}, u32[]{:S(2)}, u32[]{:S(2)}) collective-permute-start(bf16[1024,256]{1,0:T(8,128)(2,1)S(1)} %collective-permute-done.16.refs_9_), channel_id=1, source_target_pairs={{0,1},{1,0},{2,3},{3,2},{4,5},{5,4},{6,7},{7,6},{8,9},{9,8},{10,11... | collective-permute-start | bytes 1572872 | tf_op jit(solution)/shard_map/ppermute | solution.py:413
  105.6 3.2 %copy-start.6 = (bf16[2,2,128,128]{3,2,1,0:T(8,128)(2,1)}, bf16[2,2,128,128]{3,2,1,0:T(8,128)(2,1)S(1)}, u32[]{:S(2)}) copy-start(bf16[2,2,128,128]{3,2,1,0:T(8,128)(2,1)S(1)} %collective-permute-done.10.refs_2_) | copy-start | bytes 393220
  105.6 25.9 %collective-permute-start.21 = (bf16[1024,256]{1,0:T(8,128)(2,1)}, bf16[1024,256]{1,0:T(8,128)(2,1)}, u32[]{:S(2)}, u32[]{:S(2)}) collective-permute-start(bf16[1024,256]{1,0:T(8,128)(2,1)} %collective-permute-done.17.refs_10_), channel_id=1, source_target_pairs={{0,1},{1,0},{2,3},{3,2},{4,5},{5,4},{6,7},{7,6},{8,9},{9,8},{10,11... | collective-permute-start | bytes 1572872 | tf_op jit(solution)/shard_map/ppermute | solution.py:413
  108.9 0.7 copy-start.7
  109.5 22.1 %collective-permute-start.22 = (bf16[1024,256]{1,0:T(8,128)(2,1)}, bf16[1024,256]{1,0:T(8,128)(2,1)}, u32[]{:S(2)}, u32[]{:S(2)}) collective-permute-start(bf16[1024,256]{1,0:T(8,128)(2,1)} %collective-permute-done.18.refs_11_), channel_id=1, source_target_pairs={{0,1},{1,0},{2,3},{3,2},{4,5},{5,4},{6,7},{7,6},{8,9},{9,8},{10,11... | collective-permute-start | bytes 1572872 | tf_op jit(solution)/shard_map/ppermute | solution.py:413
  110.9 20.6 %all-to-all-start.3 = ((bf16[32,32,128]{2,1,0:T(8,128)(2,1)}), bf16[32,32,128]{2,1,0:T(8,128)(2,1)S(1)}, u32[]{:S(2)}, u32[]{:S(2)}) async-start(bf16[32,32,128]{2,1,0:T(8,128)(2,1)} %earlier.1), calls=%async_computation.3 | async-start | bytes 524288 | tf_op jit(solution)/shard_map/all_to_all | solution.py:432
  119.5 1.4 %collective-permute-start.13 = (bf16[2,2,128,128]{3,2,1,0:T(8,128)(2,1)S(1)}, bf16[2,2,128,128]{3,2,1,0:T(8,128)(2,1)S(1)}, u32[]{:S(2)}, u32[]{:S(2)}) collective-permute-start(bf16[2,2,128,128]{3,2,1,0:T(8,128)(2,1)S(1)} %collective-permute-done.9.refs_1_), channel_id=1, source_target_pairs={{0,1},{1,0},{2,3},{3,2},{4,5},{5,4},{6,7},{7,6},{8,9},{9,8},{10,11... | collective-permute-start | bytes 393224 | tf_op jit(solution)/shard_map/ppermute | solution.py:413
  121.0 0.7 copy-start.8
  121.6 1.7 %collective-permute-start.14 = (bf16[2,2,128,128]{3,2,1,0:T(8,128)(2,1)}, bf16[2,2,128,128]{3,2,1,0:T(8,128)(2,1)}, u32[]{:S(2)}, u32[]{:S(2)}) collective-permute-start(bf16[2,2,128,128]{3,2,1,0:T(8,128)(2,1)} %copy-done.6), channel_id=1, source_target_pairs={{0,1},{1,0},{2,3},{3,2},{4,5},{5,4},{6,7},{7,6},{8,9},{9,8},{10,11... | collective-permute-start | bytes 393224 | tf_op jit(solution)/shard_map/ppermute | solution.py:413
  123.3 1.7 %collective-permute-start.15 = (bf16[2,2,128,128]{3,2,1,0:T(8,128)(2,1)}, bf16[2,2,128,128]{3,2,1,0:T(8,128)(2,1)}, u32[]{:S(2)}, u32[]{:S(2)}) collective-permute-start(bf16[2,2,128,128]{3,2,1,0:T(8,128)(2,1)} %copy-done.7), channel_id=1, source_target_pairs={{0,1},{1,0},{2,3},{3,2},{4,5},{5,4},{6,7},{7,6},{8,9},{9,8},{10,11... | collective-permute-start | bytes 393224 | tf_op jit(solution)/shard_map/ppermute | solution.py:413
  131.5 0.7 copy-start.3
where the time goes:
time: 141 us; the launch traced here: 140 us
  starting transfers between devices  63.8 us (45%)
  waiting for transfers between devices  36 us (26%)
  Pallas kernels  29.6 us (21%)
  local copies, waits for them, and re-layouts  9.2 us (7%)
    ppermute x13, starting transfers between devices, partner_of(): return lax.ppermute(block, 'seq', swap)  18.2 us
    pallas_call x1, Pallas kernels, attend(): pl.pallas_call(attend_kernel, out_shape=(block,) * groups + (jax.ShapeDty...  15.2 us
    ppermute x10, starting transfers between devices, along_ring(): lax.ppermute(block, 'seq', [(i, (i + 2 * by) % fields) for i in range(fie...  14.4 us
    all_to_all x1, waiting for transfers between devices, gather_depth(): lax.all_to_all(blocks, 'step', 0, 0, axis_index_groups=[[x + shape[1] * z...  12.8 us
    ppermute x10, waiting for transfers between devices, along_ring(): lax.ppermute(block, 'seq', [(i, (i + 2 * by) % fields) for i in range(fie...  10.8 us
    all_to_all x1, starting transfers between devices, local(): lax.all_to_all(sums.reshape(groups * fields, per, pair), ('step', 'seq'),...  9.09 us
    all_to_all x1, starting transfers between devices, gather_depth(): lax.all_to_all(blocks, 'step', 0, 0, axis_index_groups=[[x + shape[1] * z...  9.01 us
    all_to_all x1, starting transfers between devices, local(): before = lax.all_to_all(earlier(received), 'step', 0, 0)  8.62 us
  transfers between devices with their start and end apart: 27, of which 9 were waited for; matrix products, arithmetic and copies ran while one was open for 5% of the time, Pallas kernels for 14%

commit v1 on v0

--- a/solution.py
+++ b/solution.py
@@ -80,42 +80,27 @@
     )(shift, gain, rows)
 
 
-def tile_kernel(source_ref, tile_ref, half_ref, sems):
-    pair = half_ref.shape[-1]
-    across = half_ref.shape[0]
-    start = source_ref.shape[-1] - pair
-    loads = [
-        pltpu.make_async_copy(
-            source_ref.at[x, :, :, pl.ds(start, pair)], half_ref.at[x], sems.at[x]
-        )
-        for x in range(across)
-    ]
-    for load in loads:
-        load.start()
-    low = tile_ref.shape[2]
-    for x, load in enumerate(loads):
-        load.wait()
+def tile_kernel(place_ref, *refs):
+    sources, tile_ref = refs[:-1], refs[-1]
+    low, pair = tile_ref.shape[2], sources[0].shape[-1]
+    for k, ref in enumerate(sources):
         for half in range(2):
-            tile_ref[:, x, :, half * pair : (half + 1) * pair] = half_ref[
-                x, :, half * low : (half + 1) * low
+            tile_ref[:, place_ref[1 + k], :, half * pair : (half + 1) * pair] = ref[
+                :, half * low : (half + 1) * low
             ]
 
 
-def tile_of(weights):
-    across, depth, height, columns = weights.shape
-    pair = columns // 4
+def tile_of(place, sources):
+    depth, height, pair = sources[0].shape
+    across = len(sources)
     return pl.pallas_call(
         tile_kernel,
         out_shape=jax.ShapeDtypeStruct((depth, across, height // 2, 2 * pair), BF16),
-        in_specs=[HBM],
+        in_specs=[SMEM] + [VMEM] * across,
         out_specs=VMEM,
-        scratch_shapes=[
-            pltpu.VMEM((across, depth, height, pair), BF16),
-            pltpu.SemaphoreType.DMA((across,)),
-        ],
         compiler_params=pltpu.CompilerParams(vmem_limit_bytes=60 * MIB),
         name="tile",
-    )(weights).reshape(-1, 2 * pair)
+    )(place, *sources).reshape(-1, 2 * pair)
 
 
 def attend_kernel(place_ref, sizes_ref, source_ref, *refs):
@@ -182,7 +167,7 @@
                 load.wait()
             start(unit + 4)
             part = jnp.dot(
-                rows_ref[step, group], weight[:, : 3 * pair], preferred_element_type=F32
+                rows_ref[step, group], weight[...], preferred_element_type=F32
             ).astype(BF16)
             span = slice(group * rows, (group + 1) * rows)
             parts_ref[span, :] = part[:, :pair]
@@ -202,7 +187,7 @@
             attended = jnp.where(first, heads[0], heads[1]).astype(BF16)
             for side in range(2):
                 block = attended[side * half : (side + 1) * half]
-                spot = place_ref[2 * position + side]
+                spot = place_ref[5 + 2 * position + side]
                 outs[position][side, step] = block
                 scaled = sizes_ref[step] * block.astype(F32)
                 if step == 0:
@@ -222,7 +207,7 @@
 def attend(place, sizes, weights, blocks, targets):
     steps, half, width = blocks[0].shape
     across, depth, height, columns = weights.shape
-    pair = columns // 4
+    pair = columns // 3
     groups, rows = 4, 2 * half
     length = groups * rows
     block = jax.ShapeDtypeStruct((2, steps, half, pair), BF16)
@@ -272,7 +257,7 @@
     )(sums)
 
 
-def total_kernel(place_ref, heads_ref, sizes_ref, before_ref, initial_ref, *refs):
+def total_kernel(place_ref, sizes_ref, before_ref, initial_ref, *refs):
     blocks, tiles = refs[:8], refs[8:16]
     out_ref, order_ref, rows_ref, weight_ref, result_ref, load_sems, store_sems = refs[16:]
     groups, depth, pair = before_ref.shape
@@ -283,7 +268,7 @@
         pltpu.make_async_copy(source, weight_ref.at[index], load_sems.at[index])
         for index, source in enumerate(tiles)
     ]
-    for load in loads[:3]:
+    for load in loads:
         load.start()
 
     order_ref[...] = before_ref[...].astype(F32).reshape(order_ref.shape)
@@ -294,18 +279,17 @@
                 pl.ds(per * field + turn, groups, stride=depth), :
             ].astype(BF16)
     for index, ref in enumerate(blocks):
-        start = pl.multiple_of(heads_ref[index] * pair, pair)
+        start = pl.multiple_of(place_ref[21 + index] * pair, pair)
         for step in range(2):
             rows_ref[(1 + step) * rows : (2 + step) * rows, pl.ds(start, pair)] = ref[
                 index // 4, step
             ]
 
+    for load in loads:
+        load.wait()
     stores = []
-    for index, load in enumerate(loads):
-        load.wait()
-        for later in loads[index + 3 : index + 4]:
-            later.start()
-        start = pl.multiple_of(place_ref[index] * width, width)
+    for index in range(len(loads)):
+        start = pl.multiple_of(place_ref[13 + index] * width, width)
         drift = jnp.dot(rows_ref[...], weight_ref[index], preferred_element_type=F32)
         base = (
             initial_ref[:, pl.ds(start, width)].astype(F32)
@@ -323,14 +307,14 @@
         store.wait()
 
 
-def totals(place, heads, sizes, before, initial, blocks, tiles):
+def totals(place, sizes, before, initial, blocks, tiles):
     rows, width = initial.shape
     groups, depth, pair = before.shape
     count = len(tiles)
     return pl.pallas_call(
         total_kernel,
         out_shape=jax.ShapeDtypeStruct((2, rows, width), F32),
-        in_specs=[SMEM] * 3 + [VMEM] * 10 + [HBM] * 8,
+        in_specs=[SMEM] * 2 + [VMEM] * 10 + [HBM] * 8,
         out_specs=HBM,
         scratch_shapes=[
             pltpu.VMEM((groups * depth, pair), F32),
@@ -342,7 +326,7 @@
         ],
         compiler_params=pltpu.CompilerParams(vmem_limit_bytes=60 * MIB),
         name="totals",
-    )(place, heads, sizes, before, initial, *blocks, *tiles)
+    )(place, sizes, before, initial, *blocks, *tiles)
 
 
 def gather_depth(blocks, shape):
@@ -352,6 +336,15 @@
         0,
         0,
         axis_index_groups=[[x + shape[1] * z for z in range(shape[0])] for x in range(shape[1])],
+    )
+
+
+def fetch_column(block, shape, by):
+    across = shape[1]
+    return lax.ppermute(
+        block,
+        "step",
+        [(i, i // across * across + (i - by) % across) for i in range(shape[0] * across)],
     )
 
 
@@ -391,23 +384,35 @@
         return lax.ppermute(block, "seq", [(i, (i + 2 * by) % fields) for i in range(fields)])
 
     shifts_by = (1, chips - 1, 2)
+    column = lax.axis_index("step") % 4
+    source_chips = [chip] + [(chip - by) % chips for by in shifts_by]
+    head_chips = [chip] + [(chip + by) % chips for by in shifts_by]
+    index = jnp.stack(
+        [place]
+        + [(column + by) % 4 for by in range(4)]
+        + [spot for source in source_chips for spot in (2 * source + core, 2 * source + 1 - core)]
+        + [2 * source + core for source in source_chips]
+        + [2 * source + 1 - core for source in source_chips]
+        + [2 * source + core for source in head_chips]
+        + [2 * source + 1 - core for source in head_chips]
+    ).astype(jnp.int32)
+
     picked = pick(
-        place[None].astype(jnp.int32),
+        index,
         query_weight,
         key_weight,
         value_weight,
         out_weight,
         shape[0],
     )
-    weights = gather_columns(gather_depth(picked, shape), shape)
+    along = gather_depth(picked, shape)
+    weights = gather_columns(along[:, :, : 3 * pair], shape)
+    out_along = along[:, :, 3 * pair :]
+    out_blocks = [out_along] + [fetch_column(out_along, shape, by) for by in range(1, shape[1])]
+    out_tile = tile_of(index, out_blocks)
 
     shifts, scales = modulation(time_index, plan, adaln_weight)
     gains = 1.0 + scales
-
-    source_chips = [chip] + [(chip - by) % chips for by in shifts_by]
-    places = jnp.stack(
-        [spot for source in source_chips for spot in (2 * source + core, 2 * source + 1 - core)]
-    ).astype(jnp.int32)
 
     def partner_of(block):
         return lax.ppermute(block, "seq", swap)
@@ -418,10 +423,10 @@
     blocks = []
     for block in (here, behind, ahead):
         blocks += [block, partner_of(block)]
+    opposite, out_tile = lax.optimization_barrier((opposite, out_tile))
     blocks += opposite + [partner_of(block) for block in opposite]
-    out_tile = tile_of(weights)
     out_tiles = [out_tile] + [along_ring(out_tile, by) for by in shifts_by]
-    attended, sums = attend(places, step_sizes, weights, blocks, groups)
+    attended, sums = attend(index, step_sizes, weights, blocks, groups)
     out_tiles, _ = lax.optimization_barrier((out_tiles, sums))
     out_tiles = out_tiles + [partner_of(tile) for tile in out_tiles]
 
@@ -435,12 +440,7 @@
         along_ring(block, chips - by) for block, by in zip(attended[1:], shifts_by)
     ]
     arrived = arrived + [partner_of(block) for block in arrived]
-    sources = [chip] + [(chip + by) % chips for by in shifts_by]
-    heads = jnp.stack(
-        [2 * source + core for source in sources] + [2 * source + 1 - core for source in sources]
-    ).astype(jnp.int32)
-    spots = jnp.concatenate([places[0::2], places[1::2]])
-    return totals(spots, heads, step_sizes, before, initial, arrived, out_tiles)
+    return totals(index, step_sizes, before, initial, arrived, out_tiles)
 
 
 def solution(mesh):

time: 141 us -> 135 us (0.957)
  waiting for transfers between devices: 36 us -> 11.8 us
  blocking collectives: 0 us -> 23.6 us
  Pallas kernels: 29.6 us -> 26.9 us
  local copies, waits for them, and re-layouts: 9.2 us -> 7.05 us
    all_to_all x0 -> x1, blocking collectives: none -> 23.6 us  [gather_depth(): lax.all_to_all(blocks, 'step', 0, 0, axis_index_groups=[[x + shape[1] * z...]
    all_to_all x1 -> x0, waiting for transfers between devices: 12.8 us -> none  [gather_depth(): lax.all_to_all(blocks, 'step', 0, 0, axis_index_groups=[[x + shape[1] * z...]
    ppermute x10, waiting for transfers between devices: 10.8 us -> 0.9 us  [along_ring(): lax.ppermute(block, 'seq', [(i, (i + 2 * by) % fields) for i in range(fie...]
    all_to_all x1 -> x0, starting transfers between devices: 9.01 us -> none  [gather_depth(): lax.all_to_all(blocks, 'step', 0, 0, axis_index_groups=[[x + shape[1] * z...]
    ppermute x0 -> x3, starting transfers between devices: none -> 3.68 us  [fetch_column(): lax.ppermute(block, 'step', [(i, i // across * across + (i - by) % across...]
    all_to_all x1, waiting for transfers between devices: 3.37 us -> 0.01 us  [gather_columns(): lax.all_to_all(jnp.broadcast_to(block[None], (across,) + block.shape), 's...]
    ppermute x13, starting transfers between devices: 18.2 us -> 21.5 us  [partner_of(): return lax.ppermute(block, 'seq', swap)]
    ppermute x13, waiting for transfers between devices: 2.5 us -> 4.28 us  [partner_of(): return lax.ppermute(block, 'seq', swap)]
  transfers between devices with their start and end apart: 27 -> 29, of which waited for: 9 -> 8; matrix products, arithmetic and copies ran while one was open for 5% -> 4% of each run, Pallas kernels for 14% -> 15%
where the time goes in v1:
time: 135 us; the launch traced here: 134 us
  starting transfers between devices  63 us (47%)
  Pallas kernels  26.9 us (20%)
  blocking collectives  23.6 us (17%)
  waiting for transfers between devices  11.8 us (9%)
  local copies, waits for them, and re-layouts  7.05 us (5%)
    all_to_all x1, blocking collectives, gather_depth(): lax.all_to_all(blocks, 'step', 0, 0, axis_index_groups=[[x + shape[1] * z...  23.6 us
    ppermute x13, starting transfers between devices, partner_of(): return lax.ppermute(block, 'seq', swap)  21.5 us
    pallas_call x1, Pallas kernels, attend(): pl.pallas_call(attend_kernel, out_shape=(block,) * groups + (jax.ShapeDty...  15 us
    ppermute x10, starting transfers between devices, along_ring(): lax.ppermute(block, 'seq', [(i, (i + 2 * by) % fields) for i in range(fie...  14.9 us
    all_to_all x1, starting transfers between devices, local(): lax.all_to_all(sums.reshape(groups * fields, per, pair), ('step', 'seq'),...  10.2 us
    all_to_all x1, starting transfers between devices, local(): before = lax.all_to_all(earlier(received), 'step', 0, 0)  8.41 us
    all_to_all x1, waiting for transfers between devices, local(): before = lax.all_to_all(earlier(received), 'step', 0, 0)  6.44 us
    pallas_call x1, Pallas kernels, totals(): pl.pallas_call(total_kernel, out_shape=jax.ShapeDtypeStruct((2, rows, wid...  6.39 us
  transfers between devices with their start and end apart: 29, of which 8 were waited for; matrix products, arithmetic and copies ran while one was open for 4% of the time, Pallas kernels for 15%

profile of v1, /device:TPU:1, one launch (start us, length us, event | category | flops | bytes accessed | tf_op | source)
XLA Modules:
  0.0 134.4 jit_solution(11301905756668720885)
XLA Ops:
  0.0 1.0 fusion
  1.1 0.1 fusion.1
  1.2 0.4 copy-done
  1.6 0.4 fusion.3
  2.0 0.8 normalize.1.refs_0_
  2.8 2.2 %collective-permute-start.1 = (bf16[2,128,2048]{2,1,0:T(8,128)(2,1)S(1)}, bf16[2,128,2048]{2,1,0:T(8,128)(2,1)}, u32[]{:S(2)}, u32[]{:S(2)}) collective-permute-start(bf16[2,128,2048]{2,1,0:T(8,128)(2,1)S(1)} %normalize.1.refs_0_), channel_id=1, source_target_pairs={{0,2},{1,3},{2,4},{3,5},{4,6},{5,7},{6,0},{7,1},{8,10},{9,11},{10,... | collective-permute-start | bytes 3145736 | tf_op jit(solution)/shard_map/ppermute | solution.py:384
  5.0 1.5 %collective-permute-start.3 = (bf16[2,128,2048]{2,1,0:T(8,128)(2,1)S(1)}, bf16[2,128,2048]{2,1,0:T(8,128)(2,1)}, u32[]{:S(2)}, u32[]{:S(2)}) collective-permute-start(bf16[2,128,2048]{2,1,0:T(8,128)(2,1)S(1)} %normalize.1.refs_0_), channel_id=1, source_target_pairs={{0,6},{1,7},{2,0},{3,1},{4,2},{5,3},{6,4},{7,5},{8,14},{9,15},{10,... | collective-permute-start | bytes 3145736 | tf_op jit(solution)/shard_map/ppermute | solution.py:384
  6.5 0.7 stack.89.place_ref
  7.2 1.9 %pick.1 = bf16[8,64,512]{2,1,0:T(8,128)(2,1)} custom-call(s32[29]{0:T(128)} %stack.89.place_ref, bf16[64,1024]{1,0:T(8,128)(2,1)} %query_ref.1, bf16[64,1024]{1,0:T(8,128)(2,1)} %key_ref.1, bf16[64,1024]{1,0:T(8,128)(2,1)} %value_ref.1, bf16[32,2048]{1,0:T(8,128)(2,1)} %out_weight_ref.1), custom_call_target="tpu_custom_call" | custom-call | tf_op jit(solution)/shard_map/pick/pallas_call | solution.py:48
  9.1 23.6 %all_to_all.20 = bf16[8,64,512]{2,1,0:T(8,128)(2,1)S(1)} all-to-all(bf16[8,64,512]{2,1,0:T(8,128)(2,1)} %pick.1), channel_id=1, replica_groups={{0,32,64,96,128,160,192,224},{8,40,72,104,136,168,200,232},{16,48,80,11..., dimensions={0} | all-to-all | bytes 1048576 | tf_op jit(solution)/shard_map/all_to_all | solution.py:333
  32.8 2.6 %collective-permute-start.7 = (bf16[8,64,128]{2,1,0:T(8,128)(2,1)S(1)}, bf16[8,64,128]{2,1,0:T(8,128)(2,1)S(1)}, u32[]{:S(2)}, u32[]{:S(2)}) collective-permute-start(bf16[8,64,128]{2,1,0:T(8,128)(2,1)S(1)} %slice.29.refs_0_), channel_id=1, source_target_pairs={{0,24},{8,0},{16,8},{24,16},{32,56},{40,32},{48,40},{56,48},{64,88... | collective-permute-start | bytes 393224 | tf_op jit(solution)/shard_map/ppermute | solution.py:344
  35.4 0.5 collective-permute-start.8
  35.9 0.6 collective-permute-start.9
  36.6 1.4 %broadcast_in_dim.2 = bf16[4,8,64,384]{3,2,1,0:T(8,128)(2,1)} broadcast(bf16[8,64,384]{2,1,0:T(8,128)(2,1)S(1)} %slice.24), dimensions={1,2,3} | broadcast | bytes 1966080 | tf_op jit(solution)/shard_map/broadcast_in_dim | solution.py:354
  38.0 4.3 %all-to-all-start.1 = ((bf16[4,8,64,384]{3,2,1,0:T(8,128)(2,1)}), bf16[4,8,64,384]{3,2,1,0:T(8,128)(2,1)}, u32[]{:S(2)}, u32[]{:S(2)}) async-start(bf16[4,8,64,384]{3,2,1,0:T(8,128)(2,1)} %broadcast_in_dim.2), calls=%async_computation.1 | async-start | bytes 3145728 | tf_op jit(solution)/shard_map/all_to_all | solution.py:353
  42.3 1.1 slice.27
  43.4 0.1 collective-permute-start.5
  43.5 1.9 %slice.28 = bf16[1,128,2048]{2,1,0:T(8,128)(2,1)} slice(bf16[2,128,2048]{2,1,0:T(8,128)(2,1)} %collective-permute-done.3.refs_4_), slice={[1:2], [0:128], [0:2048]} | slice | bytes 1048576 | tf_op jit(solution)/shard_map/slice | solution.py:422
  45.4 2.7 %collective-permute-start.6 = (bf16[1,128,2048]{2,1,0:T(8,128)(2,1)}, bf16[1,128,2048]{2,1,0:T(8,128)(2,1)}, u32[]{:S(2)}, u32[]{:S(2)}) collective-permute-start(bf16[1,128,2048]{2,1,0:T(8,128)(2,1)} %slice.28), channel_id=1, source_target_pairs={{0,6},{1,7},{2,0},{3,1},{4,2},{5,3},{6,4},{7,5},{8,14},{9,15},{10,... | collective-permute-start | bytes 1572872 | tf_op jit(solution)/shard_map/ppermute | solution.py:384
  48.1 0.0 collective-permute-done.7.refs_1_
  48.1 4.5 %collective-permute-start = (bf16[2,128,2048]{2,1,0:T(8,128)(2,1)S(1)}, bf16[2,128,2048]{2,1,0:T(8,128)(2,1)}, u32[]{:S(2)}, u32[]{:S(2)}) collective-permute-start(bf16[2,128,2048]{2,1,0:T(8,128)(2,1)S(1)} %normalize.1.refs_0_), channel_id=1, source_target_pairs={{0,1},{1,0},{2,3},{3,2},{4,5},{5,4},{6,7},{7,6},{8,9},{9,8},{10,11... | collective-permute-start | bytes 3145736 | tf_op jit(solution)/shard_map/ppermute | solution.py:418
  52.6 0.1 collective-permute-start.2
  52.7 0.0 collective-permute-done.9.refs_3_
  52.7 0.4 collective-permute-start.4
  53.1 0.1 copy-done.13
  53.2 2.0 %tile.1 = bf16[8,4,32,256]{3,2,1,0:T(8,128)(2,1)} custom-call(s32[29]{0:T(128)} %stack.89.place_ref, bf16[8,64,128]{2,1,0:T(8,128)(2,1)} %copy-done.5, bf16[8,64,128]{2,1,0:T(8,128)(2,1)} %copy-done.12, bf16[8,64,128]{2,1,0:T(8,128)(2,1)} %copy-done.13, bf16[8,64,128]{2,1,0:T(8,128)(2,1)} %collective-permute-done.9.refs_3_), custom_call_target="tpu_custom_call" | custom-call | tf_op jit(solution)/shard_map/tile/pallas_call | solution.py:96
  55.2 0.3 collective-permute-done.6.refs_7_
  55.5 5.0 %collective-permute-start.10 = (bf16[1,128,2048]{2,1,0:T(8,128)(2,1)}, bf16[1,128,2048]{2,1,0:T(8,128)(2,1)}, u32[]{:S(2)}, u32[]{:S(2)}) collective-permute-start(bf16[1,128,2048]{2,1,0:T(8,128)(2,1)} %collective-permute-done.5.refs_6_), channel_id=1, source_target_pairs={{0,1},{1,0},{2,3},{3,2},{4,5},{5,4},{6,7},{7,6},{8,9},{9,8},{10,11... | collective-permute-start | bytes 1572872 | tf_op jit(solution)/shard_map/ppermute | solution.py:418
  60.5 0.6 collective-permute-start.19
  61.1 1.3 collective-permute-done.10.refs_8_
  62.4 3.4 %collective-permute-start.20 = (bf16[1024,256]{1,0:T(8,128)(2,1)}, bf16[1024,256]{1,0:T(8,128)(2,1)}, u32[]{:S(2)}, u32[]{:S(2)}) collective-permute-start(bf16[1024,256]{1,0:T(8,128)(2,1)} %bitcast.25), channel_id=1, source_target_pairs={{0,6},{1,7},{2,0},{3,1},{4,2},{5,3},{6,4},{7,5},{8,14},{9,15},{10,... | collective-permute-start | bytes 1572872 | tf_op jit(solution)/shard_map/ppermute | solution.py:384
  65.8 0.0 collective-permute-start.21
  65.8 0.0 collective-permute-done.2.refs_3_
  65.8 0.0 collective-permute-done.4.refs_5_
  65.9 15.0 %attend.1 = (bf16[2,2,128,128]{3,2,1,0:T(8,128)(2,1)}, bf16[2,2,128,128]{3,2,1,0:T(8,128)(2,1)}, bf16[2,2,128,128]{3,2,1,0:T(8,128)(2,1)}, bf16[2,2,128,128]{3,2,1,0:T(8,128)(2,1)}, bf16[32,32,128]{2,1,0:T(8,128)(2,1)}) custom-call(s32[29]{0:T(128)} %stack.89.place_ref, f32[2]{0:T(128)} %sizes_ref.3, bf16[4,8,64,384]{3,2,1,0:T(8,128)(2,1)} %all-to-all-done.1.source_ref, ...), custom_call_target="tpu_custom_call" | custom-call | flops 5368709120 | bytes 10485760 | tf_op jit(solution)/shard_map/attend/pallas_call | solution.py:214
  80.9 10.2 %all-to-all-start.2 = ((bf16[256,4,128]{2,1,0:T(4,128)(2,1)}), bf16[256,4,128]{2,1,0:T(4,128)(2,1)S(1)}, u32[]{:S(2)}, u32[]{:S(2)}) async-start(bf16[256,4,128]{2,1,0:T(4,128)(2,1)} %bitcast.29), calls=%async_computation.2 | async-start | bytes 524288 | tf_op jit(solution)/shard_map/all_to_all | solution.py:434
  91.1 2.7 %collective-permute-start.12 = (bf16[2,2,128,128]{3,2,1,0:T(8,128)(2,1)}, bf16[2,2,128,128]{3,2,1,0:T(8,128)(2,1)S(1)}, u32[]{:S(2)}, u32[]{:S(2)}) collective-permute-start(bf16[2,2,128,128]{3,2,1,0:T(8,128)(2,1)} %get-tuple-element.21), channel_id=1, source_target_pairs={{0,6},{1,7},{2,0},{3,1},{4,2},{5,3},{6,4},{7,5},{8,14},{9,15},{10,... | collective-permute-start | bytes 393224 | tf_op jit(solution)/shard_map/ppermute | solution.py:384
  93.9 0.0 collective-permute-done.19.refs_9_
  93.9 1.7 %collective-permute-start.14 = (bf16[2,2,128,128]{3,2,1,0:T(8,128)(2,1)}, bf16[2,2,128,128]{3,2,1,0:T(8,128)(2,1)S(1)}, u32[]{:S(2)}, u32[]{:S(2)}) collective-permute-start(bf16[2,2,128,128]{3,2,1,0:T(8,128)(2,1)} %get-tuple-element.23), channel_id=1, source_target_pairs={{0,4},{1,5},{2,6},{3,7},{4,0},{5,1},{6,2},{7,3},{8,12},{9,13},{10,... | collective-permute-start | bytes 393224 | tf_op jit(solution)/shard_map/ppermute | solution.py:384
  95.6 0.0 collective-permute-done.20.refs_10_
  95.6 0.0 collective-permute-done.21.refs_11_
  95.6 1.2 collective-permute-start.22
  96.8 0.1 collective-permute-start.15
  96.9 0.6 collective-permute-done.12.refs_1_
  97.5 5.4 %collective-permute-start.23 = (bf16[1024,256]{1,0:T(8,128)(2,1)S(1)}, bf16[1024,256]{1,0:T(8,128)(2,1)}, u32[]{:S(2)}, u32[]{:S(2)}) collective-permute-start(bf16[1024,256]{1,0:T(8,128)(2,1)S(1)} %collective-permute-done.19.refs_9_), channel_id=1, source_target_pairs={{0,1},{1,0},{2,3},{3,2},{4,5},{5,4},{6,7},{7,6},{8,9},{9,8},{10,11... | collective-permute-start | bytes 1572872 | tf_op jit(solution)/shard_map/ppermute | solution.py:418
  102.9 0.0 collective-permute-done.13.refs_2_
  102.9 3.2 %collective-permute-start.24 = (bf16[1024,256]{1,0:T(8,128)(2,1)}, bf16[1024,256]{1,0:T(8,128)(2,1)}, u32[]{:S(2)}, u32[]{:S(2)}) collective-permute-start(bf16[1024,256]{1,0:T(8,128)(2,1)} %collective-permute-done.20.refs_10_), channel_id=1, source_target_pairs={{0,1},{1,0},{2,3},{3,2},{4,5},{5,4},{6,7},{7,6},{8,9},{9,8},{10,11... | collective-permute-start | bytes 1572872 | tf_op jit(solution)/shard_map/ppermute | solution.py:418
  106.1 0.1 collective-permute-start.25
  106.2 0.2 all-to-all-done.2
  106.4 0.7 earlier.1
  107.1 8.4 %all-to-all-start.3 = ((bf16[32,32,128]{2,1,0:T(8,128)(2,1)}), bf16[32,32,128]{2,1,0:T(8,128)(2,1)S(1)}, u32[]{:S(2)}, u32[]{:S(2)}) async-start(bf16[32,32,128]{2,1,0:T(8,128)(2,1)} %earlier.1), calls=%async_computation.3 | async-start | bytes 524288 | tf_op jit(solution)/shard_map/all_to_all | solution.py:437
  115.5 0.0 collective-permute-done.15.refs_4_
  115.5 0.8 collective-permute-start.16
  116.3 1.0 collective-permute-done.16.refs_5_
  117.3 0.4 collective-permute-start.17
  117.7 1.0 collective-permute-done.17.refs_6_
  118.7 0.4 collective-permute-start.18
  119.0 1.0 collective-permute-done.18.refs_7_
  120.0 0.0 collective-permute-done.22.refs_12_
  120.0 0.0 collective-permute-done.23.refs_13_
  120.0 0.6 copy-done.11
  120.7 6.4 %all-to-all-done.3.before_ref = bf16[32,32,128]{2,1,0:T(8,128)(2,1)S(1)} async-done(((bf16[32,32,128]{2,1,0:T(8,128)(2,1)}), bf16[32,32,128]{2,1,0:T(8,128)(2,1)S(1)}, u32[]{:S(2)}, u32[]{:S(2)}) %all-to-all-start.3) | async-done | bytes 262176 | tf_op jit(solution)/shard_map/all_to_all | solution.py:437
  127.2 0.7 copy-done.3
  127.8 6.4 %totals.1 = f32[2,128,2048]{2,1,0:T(8,128)} custom-call(s32[29]{0:T(128)} %stack.89.place_ref, f32[2]{0:T(128)} %sizes_ref.3, bf16[32,32,128]{2,1,0:T(8,128)(2,1)} %copy-done.3, bf16[128,2048]{1,0:T(8,128)(2,1)} %initial_ref.1, bf16[2,2,128,128]{3,2,1,0:T(8,128)(2,1)} %get-tuple-element.20.refs_0_, bf16[2,2,128,128]{3,2,1,0:T(8,128)(2,1)} %copy-done.6, ...), custom_call_target="tpu_custom_call" | custom-call | tf_op jit(solution)/shard_map/totals/pallas_call | solution.py:314
  (41 shorter events, 0.2 us)
Async XLA Ops:
  0.0 1.6 %copy-start = (bf16[256,4096]{1,0:T(8,128)(2,1)S(1)}, bf16[256,4096]{1,0:T(8,128)(2,1)}, u32[]{:S(2)}) copy-start(bf16[256,4096]{1,0:T(8,128)(2,1)} %param.15) | copy-start | bytes 6291460
  0.0 2.0 %copy-start.1 = (bf16[2,128,2048]{2,1,0:T(8,128)(2,1)S(1)}, bf16[2,128,2048]{2,1,0:T(8,128)(2,1)}, u32[]{:S(2)}) copy-start(bf16[2,128,2048]{2,1,0:T(8,128)(2,1)} %rows_ref.1) | copy-start | bytes 3145732
  2.8 45.3 %copy-start.2 = (bf16[2,128,2048]{2,1,0:T(8,128)(2,1)}, bf16[2,128,2048]{2,1,0:T(8,128)(2,1)S(1)}, u32[]{:S(2)}) copy-start(bf16[2,128,2048]{2,1,0:T(8,128)(2,1)S(1)} %normalize.1.refs_0_) | copy-start | bytes 3145732
  2.8 39.5 %collective-permute-start.1 = (bf16[2,128,2048]{2,1,0:T(8,128)(2,1)S(1)}, bf16[2,128,2048]{2,1,0:T(8,128)(2,1)}, u32[]{:S(2)}, u32[]{:S(2)}) collective-permute-start(bf16[2,128,2048]{2,1,0:T(8,128)(2,1)S(1)} %normalize.1.refs_0_), channel_id=1, source_target_pairs={{0,2},{1,3},{2,4},{3,5},{4,6},{5,7},{6,0},{7,1},{8,10},{9,11},{10,... | collective-permute-start | bytes 3145736 | tf_op jit(solution)/shard_map/ppermute | solution.py:384
  5.0 38.5 %collective-permute-start.3 = (bf16[2,128,2048]{2,1,0:T(8,128)(2,1)S(1)}, bf16[2,128,2048]{2,1,0:T(8,128)(2,1)}, u32[]{:S(2)}, u32[]{:S(2)}) collective-permute-start(bf16[2,128,2048]{2,1,0:T(8,128)(2,1)S(1)} %normalize.1.refs_0_), channel_id=1, source_target_pairs={{0,6},{1,7},{2,0},{3,1},{4,2},{5,3},{6,4},{7,5},{8,14},{9,15},{10,... | collective-permute-start | bytes 3145736 | tf_op jit(solution)/shard_map/ppermute | solution.py:384
  32.8 5.1 %copy-start.5 = (bf16[8,64,128]{2,1,0:T(8,128)(2,1)}, bf16[8,64,128]{2,1,0:T(8,128)(2,1)S(1)}, u32[]{:S(2)}) copy-start(bf16[8,64,128]{2,1,0:T(8,128)(2,1)S(1)} %slice.29.refs_0_) | copy-start | bytes 393220
  32.8 15.3 %collective-permute-start.7 = (bf16[8,64,128]{2,1,0:T(8,128)(2,1)S(1)}, bf16[8,64,128]{2,1,0:T(8,128)(2,1)S(1)}, u32[]{:S(2)}, u32[]{:S(2)}) collective-permute-start(bf16[8,64,128]{2,1,0:T(8,128)(2,1)S(1)} %slice.29.refs_0_), channel_id=1, source_target_pairs={{0,24},{8,0},{16,8},{24,16},{32,56},{40,32},{48,40},{56,48},{64,88... | collective-permute-start | bytes 393224 | tf_op jit(solution)/shard_map/ppermute | solution.py:344
  35.4 17.2 %collective-permute-start.8 = (bf16[8,64,128]{2,1,0:T(8,128)(2,1)S(1)}, bf16[8,64,128]{2,1,0:T(8,128)(2,1)S(1)}, u32[]{:S(2)}, u32[]{:S(2)}) collective-permute-start(bf16[8,64,128]{2,1,0:T(8,128)(2,1)S(1)} %slice.29.refs_0_), channel_id=1, source_target_pairs={{0,16},{8,24},{16,0},{24,8},{32,48},{40,56},{48,32},{56,40},{64,80... | collective-permute-start | bytes 393224 | tf_op jit(solution)/shard_map/ppermute | solution.py:344
  35.9 16.8 %collective-permute-start.9 = (bf16[8,64,128]{2,1,0:T(8,128)(2,1)S(1)}, bf16[8,64,128]{2,1,0:T(8,128)(2,1)}, u32[]{:S(2)}, u32[]{:S(2)}) collective-permute-start(bf16[8,64,128]{2,1,0:T(8,128)(2,1)S(1)} %slice.29.refs_0_), channel_id=1, source_target_pairs={{0,8},{8,16},{16,24},{24,0},{32,40},{40,48},{48,56},{56,32},{64,72... | collective-permute-start | bytes 393224 | tf_op jit(solution)/shard_map/ppermute | solution.py:344
  38.0 27.9 %all-to-all-start.1 = ((bf16[4,8,64,384]{3,2,1,0:T(8,128)(2,1)}), bf16[4,8,64,384]{3,2,1,0:T(8,128)(2,1)}, u32[]{:S(2)}, u32[]{:S(2)}) async-start(bf16[4,8,64,384]{3,2,1,0:T(8,128)(2,1)} %broadcast_in_dim.2), calls=%async_computation.1 | async-start | bytes 3145728 | tf_op jit(solution)/shard_map/all_to_all | solution.py:353
  43.4 11.8 %collective-permute-start.5 = (bf16[1,128,2048]{2,1,0:T(8,128)(2,1)S(1)}, bf16[1,128,2048]{2,1,0:T(8,128)(2,1)}, u32[]{:S(2)}, u32[]{:S(2)}) collective-permute-start(bf16[1,128,2048]{2,1,0:T(8,128)(2,1)S(1)} %slice.27), channel_id=1, source_target_pairs={{0,2},{1,3},{2,4},{3,5},{4,6},{5,7},{6,0},{7,1},{8,10},{9,11},{10,... | collective-permute-start | bytes 1572872 | tf_op jit(solution)/shard_map/ppermute | solution.py:384
  45.4 10.1 %collective-permute-start.6 = (bf16[1,128,2048]{2,1,0:T(8,128)(2,1)}, bf16[1,128,2048]{2,1,0:T(8,128)(2,1)}, u32[]{:S(2)}, u32[]{:S(2)}) collective-permute-start(bf16[1,128,2048]{2,1,0:T(8,128)(2,1)} %slice.28), channel_id=1, source_target_pairs={{0,6},{1,7},{2,0},{3,1},{4,2},{5,3},{6,4},{7,5},{8,14},{9,15},{10,... | collective-permute-start | bytes 1572872 | tf_op jit(solution)/shard_map/ppermute | solution.py:384
  48.1 5.0 %copy-start.12 = (bf16[8,64,128]{2,1,0:T(8,128)(2,1)}, bf16[8,64,128]{2,1,0:T(8,128)(2,1)S(1)}, u32[]{:S(2)}) copy-start(bf16[8,64,128]{2,1,0:T(8,128)(2,1)S(1)} %collective-permute-done.7.refs_1_) | copy-start | bytes 393220
  48.1 12.5 %collective-permute-start = (bf16[2,128,2048]{2,1,0:T(8,128)(2,1)S(1)}, bf16[2,128,2048]{2,1,0:T(8,128)(2,1)}, u32[]{:S(2)}, u32[]{:S(2)}) collective-permute-start(bf16[2,128,2048]{2,1,0:T(8,128)(2,1)S(1)} %normalize.1.refs_0_), channel_id=1, source_target_pairs={{0,1},{1,0},{2,3},{3,2},{4,5},{5,4},{6,7},{7,6},{8,9},{9,8},{10,11... | collective-permute-start | bytes 3145736 | tf_op jit(solution)/shard_map/ppermute | solution.py:418
  52.6 0.6 copy-start.13
  52.6 13.3 %collective-permute-start.2 = (bf16[2,128,2048]{2,1,0:T(8,128)(2,1)}, bf16[2,128,2048]{2,1,0:T(8,128)(2,1)}, u32[]{:S(2)}, u32[]{:S(2)}) collective-permute-start(bf16[2,128,2048]{2,1,0:T(8,128)(2,1)} %collective-permute-done.1.refs_2_), channel_id=1, source_target_pairs={{0,1},{1,0},{2,3},{3,2},{4,5},{5,4},{6,7},{7,6},{8,9},{9,8},{10,11... | collective-permute-start | bytes 3145736 | tf_op jit(solution)/shard_map/ppermute | solution.py:418
  52.7 13.2 %collective-permute-start.4 = (bf16[2,128,2048]{2,1,0:T(8,128)(2,1)}, bf16[2,128,2048]{2,1,0:T(8,128)(2,1)}, u32[]{:S(2)}, u32[]{:S(2)}) collective-permute-start(bf16[2,128,2048]{2,1,0:T(8,128)(2,1)} %collective-permute-done.3.refs_4_), channel_id=1, source_target_pairs={{0,1},{1,0},{2,3},{3,2},{4,5},{5,4},{6,7},{7,6},{8,9},{9,8},{10,11... | collective-permute-start | bytes 3145736 | tf_op jit(solution)/shard_map/ppermute | solution.py:418
  55.5 6.9 %collective-permute-start.10 = (bf16[1,128,2048]{2,1,0:T(8,128)(2,1)}, bf16[1,128,2048]{2,1,0:T(8,128)(2,1)}, u32[]{:S(2)}, u32[]{:S(2)}) collective-permute-start(bf16[1,128,2048]{2,1,0:T(8,128)(2,1)} %collective-permute-done.5.refs_6_), channel_id=1, source_target_pairs={{0,1},{1,0},{2,3},{3,2},{4,5},{5,4},{6,7},{7,6},{8,9},{9,8},{10,11... | collective-permute-start | bytes 1572872 | tf_op jit(solution)/shard_map/ppermute | solution.py:418
  60.5 5.3 %collective-permute-start.11 = (bf16[1,128,2048]{2,1,0:T(8,128)(2,1)}, bf16[1,128,2048]{2,1,0:T(8,128)(2,1)}, u32[]{:S(2)}, u32[]{:S(2)}) collective-permute-start(bf16[1,128,2048]{2,1,0:T(8,128)(2,1)} %collective-permute-done.6.refs_7_), channel_id=1, source_target_pairs={{0,1},{1,0},{2,3},{3,2},{4,5},{5,4},{6,7},{7,6},{8,9},{9,8},{10,11... | collective-permute-start | bytes 1572872 | tf_op jit(solution)/shard_map/ppermute | solution.py:418
  60.5 33.3 %collective-permute-start.19 = (bf16[1024,256]{1,0:T(8,128)(2,1)}, bf16[1024,256]{1,0:T(8,128)(2,1)S(1)}, u32[]{:S(2)}, u32[]{:S(2)}) collective-permute-start(bf16[1024,256]{1,0:T(8,128)(2,1)} %bitcast.24), channel_id=1, source_target_pairs={{0,2},{1,3},{2,4},{3,5},{4,6},{5,7},{6,0},{7,1},{8,10},{9,11},{10,... | collective-permute-start | bytes 1572872 | tf_op jit(solution)/shard_map/ppermute | solution.py:384
  62.4 33.2 %collective-permute-start.20 = (bf16[1024,256]{1,0:T(8,128)(2,1)}, bf16[1024,256]{1,0:T(8,128)(2,1)}, u32[]{:S(2)}, u32[]{:S(2)}) collective-permute-start(bf16[1024,256]{1,0:T(8,128)(2,1)} %bitcast.25), channel_id=1, source_target_pairs={{0,6},{1,7},{2,0},{3,1},{4,2},{5,3},{6,4},{7,5},{8,14},{9,15},{10,... | collective-permute-start | bytes 1572872 | tf_op jit(solution)/shard_map/ppermute | solution.py:384
  65.8 29.8 %collective-permute-start.21 = (bf16[1024,256]{1,0:T(8,128)(2,1)}, bf16[1024,256]{1,0:T(8,128)(2,1)}, u32[]{:S(2)}, u32[]{:S(2)}) collective-permute-start(bf16[1024,256]{1,0:T(8,128)(2,1)} %bitcast.26), channel_id=1, source_target_pairs={{0,4},{1,5},{2,6},{3,7},{4,0},{5,1},{6,2},{7,3},{8,12},{9,13},{10,... | collective-permute-start | bytes 1572872 | tf_op jit(solution)/shard_map/ppermute | solution.py:384
  80.9 25.5 %all-to-all-start.2 = ((bf16[256,4,128]{2,1,0:T(4,128)(2,1)}), bf16[256,4,128]{2,1,0:T(4,128)(2,1)S(1)}, u32[]{:S(2)}, u32[]{:S(2)}) async-start(bf16[256,4,128]{2,1,0:T(4,128)(2,1)} %bitcast.29), calls=%async_computation.2 | async-start | bytes 524288 | tf_op jit(solution)/shard_map/all_to_all | solution.py:434
  91.1 6.3 %collective-permute-start.12 = (bf16[2,2,128,128]{3,2,1,0:T(8,128)(2,1)}, bf16[2,2,128,128]{3,2,1,0:T(8,128)(2,1)S(1)}, u32[]{:S(2)}, u32[]{:S(2)}) collective-permute-start(bf16[2,2,128,128]{3,2,1,0:T(8,128)(2,1)} %get-tuple-element.21), channel_id=1, source_target_pairs={{0,6},{1,7},{2,0},{3,1},{4,2},{5,3},{6,4},{7,5},{8,14},{9,15},{10,... | collective-permute-start | bytes 393224 | tf_op jit(solution)/shard_map/ppermute | solution.py:384
  93.9 9.0 %collective-permute-start.13 = (bf16[2,2,128,128]{3,2,1,0:T(8,128)(2,1)}, bf16[2,2,128,128]{3,2,1,0:T(8,128)(2,1)S(1)}, u32[]{:S(2)}, u32[]{:S(2)}) collective-permute-start(bf16[2,2,128,128]{3,2,1,0:T(8,128)(2,1)} %get-tuple-element.22), channel_id=1, source_target_pairs={{0,2},{1,3},{2,4},{3,5},{4,6},{5,7},{6,0},{7,1},{8,10},{9,11},{10,... | collective-permute-start | bytes 393224 | tf_op jit(solution)/shard_map/ppermute | solution.py:384
  93.9 33.2 %copy-start.4 = (bf16[1024,256]{1,0:T(8,128)(2,1)}, bf16[1024,256]{1,0:T(8,128)(2,1)S(1)}, u32[]{:S(2)}) copy-start(bf16[1024,256]{1,0:T(8,128)(2,1)S(1)} %collective-permute-done.19.refs_9_) | copy-start | bytes 1572868
  93.9 12.2 %collective-permute-start.14 = (bf16[2,2,128,128]{3,2,1,0:T(8,128)(2,1)}, bf16[2,2,128,128]{3,2,1,0:T(8,128)(2,1)S(1)}, u32[]{:S(2)}, u32[]{:S(2)}) collective-permute-start(bf16[2,2,128,128]{3,2,1,0:T(8,128)(2,1)} %get-tuple-element.23), channel_id=1, source_target_pairs={{0,4},{1,5},{2,6},{3,7},{4,0},{5,1},{6,2},{7,3},{8,12},{9,13},{10,... | collective-permute-start | bytes 393224 | tf_op jit(solution)/shard_map/ppermute | solution.py:384
  95.6 24.4 %collective-permute-start.22 = (bf16[1024,256]{1,0:T(8,128)(2,1)}, bf16[1024,256]{1,0:T(8,128)(2,1)}, u32[]{:S(2)}, u32[]{:S(2)}) collective-permute-start(bf16[1024,256]{1,0:T(8,128)(2,1)} %bitcast.27), channel_id=1, source_target_pairs={{0,1},{1,0},{2,3},{3,2},{4,5},{5,4},{6,7},{7,6},{8,9},{9,8},{10,11... | collective-permute-start | bytes 1572872 | tf_op jit(solution)/shard_map/ppermute | solution.py:418
  96.8 18.7 %collective-permute-start.15 = (bf16[2,2,128,128]{3,2,1,0:T(8,128)(2,1)}, bf16[2,2,128,128]{3,2,1,0:T(8,128)(2,1)}, u32[]{:S(2)}, u32[]{:S(2)}) collective-permute-start(bf16[2,2,128,128]{3,2,1,0:T(8,128)(2,1)} %get-tuple-element.20.refs_0_), channel_id=1, source_target_pairs={{0,1},{1,0},{2,3},{3,2},{4,5},{5,4},{6,7},{7,6},{8,9},{9,8},{10,11... | collective-permute-start | bytes 393224 | tf_op jit(solution)/shard_map/ppermute | solution.py:418
  97.5 29.6 %copy-start.6 = (bf16[2,2,128,128]{3,2,1,0:T(8,128)(2,1)}, bf16[2,2,128,128]{3,2,1,0:T(8,128)(2,1)S(1)}, u32[]{:S(2)}) copy-start(bf16[2,2,128,128]{3,2,1,0:T(8,128)(2,1)S(1)} %collective-permute-done.12.refs_1_) | copy-start | bytes 393220
  97.5 22.5 %collective-permute-start.23 = (bf16[1024,256]{1,0:T(8,128)(2,1)S(1)}, bf16[1024,256]{1,0:T(8,128)(2,1)}, u32[]{:S(2)}, u32[]{:S(2)}) collective-permute-start(bf16[1024,256]{1,0:T(8,128)(2,1)S(1)} %collective-permute-done.19.refs_9_), channel_id=1, source_target_pairs={{0,1},{1,0},{2,3},{3,2},{4,5},{5,4},{6,7},{7,6},{8,9},{9,8},{10,11... | collective-permute-start | bytes 1572872 | tf_op jit(solution)/shard_map/ppermute | solution.py:418
  102.9 24.3 %copy-start.7 = (bf16[2,2,128,128]{3,2,1,0:T(8,128)(2,1)}, bf16[2,2,128,128]{3,2,1,0:T(8,128)(2,1)S(1)}, u32[]{:S(2)}) copy-start(bf16[2,2,128,128]{3,2,1,0:T(8,128)(2,1)S(1)} %collective-permute-done.13.refs_2_) | copy-start | bytes 393220
  102.9 17.2 %collective-permute-start.24 = (bf16[1024,256]{1,0:T(8,128)(2,1)}, bf16[1024,256]{1,0:T(8,128)(2,1)}, u32[]{:S(2)}, u32[]{:S(2)}) collective-permute-start(bf16[1024,256]{1,0:T(8,128)(2,1)} %collective-permute-done.20.refs_10_), channel_id=1, source_target_pairs={{0,1},{1,0},{2,3},{3,2},{4,5},{5,4},{6,7},{7,6},{8,9},{9,8},{10,11... | collective-permute-start | bytes 1572872 | tf_op jit(solution)/shard_map/ppermute | solution.py:418
  106.1 21.1 %copy-start.8 = (bf16[2,2,128,128]{3,2,1,0:T(8,128)(2,1)}, bf16[2,2,128,128]{3,2,1,0:T(8,128)(2,1)S(1)}, u32[]{:S(2)}) copy-start(bf16[2,2,128,128]{3,2,1,0:T(8,128)(2,1)S(1)} %collective-permute-done.14.refs_3_) | copy-start | bytes 393220
  106.1 14.6 %collective-permute-start.25 = (bf16[1024,256]{1,0:T(8,128)(2,1)}, bf16[1024,256]{1,0:T(8,128)(2,1)}, u32[]{:S(2)}, u32[]{:S(2)}) collective-permute-start(bf16[1024,256]{1,0:T(8,128)(2,1)} %collective-permute-done.21.refs_11_), channel_id=1, source_target_pairs={{0,1},{1,0},{2,3},{3,2},{4,5},{5,4},{6,7},{7,6},{8,9},{9,8},{10,11... | collective-permute-start | bytes 1572872 | tf_op jit(solution)/shard_map/ppermute | solution.py:418
  107.1 20.0 %all-to-all-start.3 = ((bf16[32,32,128]{2,1,0:T(8,128)(2,1)}), bf16[32,32,128]{2,1,0:T(8,128)(2,1)S(1)}, u32[]{:S(2)}, u32[]{:S(2)}) async-start(bf16[32,32,128]{2,1,0:T(8,128)(2,1)} %earlier.1), calls=%async_computation.3 | async-start | bytes 524288 | tf_op jit(solution)/shard_map/all_to_all | solution.py:437
  115.5 1.8 %collective-permute-start.16 = (bf16[2,2,128,128]{3,2,1,0:T(8,128)(2,1)S(1)}, bf16[2,2,128,128]{3,2,1,0:T(8,128)(2,1)S(1)}, u32[]{:S(2)}, u32[]{:S(2)}) collective-permute-start(bf16[2,2,128,128]{3,2,1,0:T(8,128)(2,1)S(1)} %collective-permute-done.12.refs_1_), channel_id=1, source_target_pairs={{0,1},{1,0},{2,3},{3,2},{4,5},{5,4},{6,7},{7,6},{8,9},{9,8},{10,11... | collective-permute-start | bytes 393224 | tf_op jit(solution)/shard_map/ppermute | solution.py:418
  117.3 9.8 %copy-start.9 = (bf16[2,2,128,128]{3,2,1,0:T(8,128)(2,1)}, bf16[2,2,128,128]{3,2,1,0:T(8,128)(2,1)S(1)}, u32[]{:S(2)}) copy-start(bf16[2,2,128,128]{3,2,1,0:T(8,128)(2,1)S(1)} %collective-permute-done.16.refs_5_) | copy-start | bytes 393220
  117.3 1.3 %collective-permute-start.17 = (bf16[2,2,128,128]{3,2,1,0:T(8,128)(2,1)S(1)}, bf16[2,2,128,128]{3,2,1,0:T(8,128)(2,1)S(1)}, u32[]{:S(2)}, u32[]{:S(2)}) collective-permute-start(bf16[2,2,128,128]{3,2,1,0:T(8,128)(2,1)S(1)} %collective-permute-done.13.refs_2_), channel_id=1, source_target_pairs={{0,1},{1,0},{2,3},{3,2},{4,5},{5,4},{6,7},{7,6},{8,9},{9,8},{10,11... | collective-permute-start | bytes 393224 | tf_op jit(solution)/shard_map/ppermute | solution.py:418
  118.7 8.5 %copy-start.10 = (bf16[2,2,128,128]{3,2,1,0:T(8,128)(2,1)}, bf16[2,2,128,128]{3,2,1,0:T(8,128)(2,1)S(1)}, u32[]{:S(2)}) copy-start(bf16[2,2,128,128]{3,2,1,0:T(8,128)(2,1)S(1)} %collective-permute-done.17.refs_6_) | copy-start | bytes 393220
  118.7 1.3 %collective-permute-start.18 = (bf16[2,2,128,128]{3,2,1,0:T(8,128)(2,1)S(1)}, bf16[2,2,128,128]{3,2,1,0:T(8,128)(2,1)S(1)}, u32[]{:S(2)}, u32[]{:S(2)}) collective-permute-start(bf16[2,2,128,128]{3,2,1,0:T(8,128)(2,1)S(1)} %collective-permute-done.14.refs_3_), channel_id=1, source_target_pairs={{0,1},{1,0},{2,3},{3,2},{4,5},{5,4},{6,7},{7,6},{8,9},{9,8},{10,11... | collective-permute-start | bytes 393224 | tf_op jit(solution)/shard_map/ppermute | solution.py:418
  120.0 0.7 copy-start.11
  127.1 0.7 copy-start.3

commit v2 on v1

--- a/solution.py
+++ b/solution.py
@@ -425,9 +425,10 @@
         blocks += [block, partner_of(block)]
     opposite, out_tile = lax.optimization_barrier((opposite, out_tile))
     blocks += opposite + [partner_of(block) for block in opposite]
-    out_tiles = [out_tile] + [along_ring(out_tile, by) for by in shifts_by]
+    out_tiles = [out_tile] + [along_ring(out_tile, by) for by in shifts_by[:2]]
     attended, sums = attend(index, step_sizes, weights, blocks, groups)
     out_tiles, _ = lax.optimization_barrier((out_tiles, sums))
+    out_tiles = out_tiles + [along_ring(out_tiles[1], 1)]
     out_tiles = out_tiles + [partner_of(tile) for tile in out_tiles]
 
     per = sums.shape[1] // fields

time: 135 us -> 136 us (level)
  transfers between devices with their start and end apart: 29 -> 29, of which waited for: 8 -> 7; matrix products, arithmetic and copies ran while one was open for 4% -> 4% of each run, Pallas kernels for 15% -> 15%
where the time goes in v2:
time: 136 us; the launch traced here: 135 us
  starting transfers between devices  62.3 us (46%)
  Pallas kernels  26.9 us (20%)
  blocking collectives  23.6 us (17%)
  waiting for transfers between devices  12.4 us (9%)
  local copies, waits for them, and re-layouts  7.79 us (6%)
    all_to_all x1, blocking collectives, gather_depth(): lax.all_to_all(blocks, 'step', 0, 0, axis_index_groups=[[x + shape[1] * z...  23.6 us
    ppermute x13, starting transfers between devices, partner_of(): return lax.ppermute(block, 'seq', swap)  21.5 us
    pallas_call x1, Pallas kernels, attend(): pl.pallas_call(attend_kernel, out_shape=(block,) * groups + (jax.ShapeDty...  15 us
    ppermute x10, starting transfers between devices, along_ring(): lax.ppermute(block, 'seq', [(i, (i + 2 * by) % fields) for i in range(fie...  15 us
    all_to_all x1, starting transfers between devices, local(): lax.all_to_all(sums.reshape(groups * fields, per, pair), ('step', 'seq'),...  9.18 us
    all_to_all x1, starting transfers between devices, local(): before = lax.all_to_all(earlier(received), 'step', 0, 0)  8.64 us
    all_to_all x1, waiting for transfers between devices, local(): before = lax.all_to_all(earlier(received), 'step', 0, 0)  7.14 us
    pallas_call x1, Pallas kernels, totals(): pl.pallas_call(total_kernel, out_shape=jax.ShapeDtypeStruct((2, rows, wid...  6.39 us
  transfers between devices with their start and end apart: 29, of which 7 were waited for; matrix products, arithmetic and copies ran while one was open for 4% of the time, Pallas kernels for 15%

profile of v2, /device:TPU:1, one launch (start us, length us, event | category | flops | bytes accessed | tf_op | source)
XLA Modules:
  0.0 135.0 jit_solution(14103317081456766853)
XLA Ops:
  0.0 1.0 fusion
  1.1 0.1 fusion.1
  1.2 0.4 copy-done
  1.6 0.4 fusion.3
  2.0 0.8 normalize.1.refs_0_
  2.8 2.2 %collective-permute-start.1 = (bf16[2,128,2048]{2,1,0:T(8,128)(2,1)S(1)}, bf16[2,128,2048]{2,1,0:T(8,128)(2,1)}, u32[]{:S(2)}, u32[]{:S(2)}) collective-permute-start(bf16[2,128,2048]{2,1,0:T(8,128)(2,1)S(1)} %normalize.1.refs_0_), channel_id=1, source_target_pairs={{0,2},{1,3},{2,4},{3,5},{4,6},{5,7},{6,0},{7,1},{8,10},{9,11},{10,... | collective-permute-start | bytes 3145736 | tf_op jit(solution)/shard_map/ppermute | solution.py:384
  5.0 1.5 %collective-permute-start.3 = (bf16[2,128,2048]{2,1,0:T(8,128)(2,1)S(1)}, bf16[2,128,2048]{2,1,0:T(8,128)(2,1)}, u32[]{:S(2)}, u32[]{:S(2)}) collective-permute-start(bf16[2,128,2048]{2,1,0:T(8,128)(2,1)S(1)} %normalize.1.refs_0_), channel_id=1, source_target_pairs={{0,6},{1,7},{2,0},{3,1},{4,2},{5,3},{6,4},{7,5},{8,14},{9,15},{10,... | collective-permute-start | bytes 3145736 | tf_op jit(solution)/shard_map/ppermute | solution.py:384
  6.5 0.7 stack.89.place_ref
  7.2 1.9 %pick.1 = bf16[8,64,512]{2,1,0:T(8,128)(2,1)} custom-call(s32[29]{0:T(128)} %stack.89.place_ref, bf16[64,1024]{1,0:T(8,128)(2,1)} %query_ref.1, bf16[64,1024]{1,0:T(8,128)(2,1)} %key_ref.1, bf16[64,1024]{1,0:T(8,128)(2,1)} %value_ref.1, bf16[32,2048]{1,0:T(8,128)(2,1)} %out_weight_ref.1), custom_call_target="tpu_custom_call" | custom-call | tf_op jit(solution)/shard_map/pick/pallas_call | solution.py:48
  9.2 23.6 %all_to_all.20 = bf16[8,64,512]{2,1,0:T(8,128)(2,1)S(1)} all-to-all(bf16[8,64,512]{2,1,0:T(8,128)(2,1)} %pick.1), channel_id=1, replica_groups={{0,32,64,96,128,160,192,224},{8,40,72,104,136,168,200,232},{16,48,80,11..., dimensions={0} | all-to-all | bytes 1048576 | tf_op jit(solution)/shard_map/all_to_all | solution.py:333
  32.9 2.6 %collective-permute-start.7 = (bf16[8,64,128]{2,1,0:T(8,128)(2,1)S(1)}, bf16[8,64,128]{2,1,0:T(8,128)(2,1)S(1)}, u32[]{:S(2)}, u32[]{:S(2)}) collective-permute-start(bf16[8,64,128]{2,1,0:T(8,128)(2,1)S(1)} %slice.29.refs_0_), channel_id=1, source_target_pairs={{0,24},{8,0},{16,8},{24,16},{32,56},{40,32},{48,40},{56,48},{64,88... | collective-permute-start | bytes 393224 | tf_op jit(solution)/shard_map/ppermute | solution.py:344
  35.4 0.5 collective-permute-start.8
  35.9 0.6 collective-permute-start.9
  36.6 1.4 %broadcast_in_dim.2 = bf16[4,8,64,384]{3,2,1,0:T(8,128)(2,1)} broadcast(bf16[8,64,384]{2,1,0:T(8,128)(2,1)S(1)} %slice.24), dimensions={1,2,3} | broadcast | bytes 1966080 | tf_op jit(solution)/shard_map/broadcast_in_dim | solution.py:354
  38.0 4.3 %all-to-all-start.1 = ((bf16[4,8,64,384]{3,2,1,0:T(8,128)(2,1)}), bf16[4,8,64,384]{3,2,1,0:T(8,128)(2,1)}, u32[]{:S(2)}, u32[]{:S(2)}) async-start(bf16[4,8,64,384]{3,2,1,0:T(8,128)(2,1)} %broadcast_in_dim.2), calls=%async_computation.1 | async-start | bytes 3145728 | tf_op jit(solution)/shard_map/all_to_all | solution.py:353
  42.3 0.0 collective-permute-done.1.refs_2_
  42.4 1.1 slice.27
  43.4 0.1 collective-permute-start.5
  43.5 0.0 collective-permute-done.3.refs_4_
  43.5 1.9 %slice.28 = bf16[1,128,2048]{2,1,0:T(8,128)(2,1)} slice(bf16[2,128,2048]{2,1,0:T(8,128)(2,1)} %collective-permute-done.3.refs_4_), slice={[1:2], [0:128], [0:2048]} | slice | bytes 1048576 | tf_op jit(solution)/shard_map/slice | solution.py:422
  45.4 2.7 %collective-permute-start.6 = (bf16[1,128,2048]{2,1,0:T(8,128)(2,1)}, bf16[1,128,2048]{2,1,0:T(8,128)(2,1)}, u32[]{:S(2)}, u32[]{:S(2)}) collective-permute-start(bf16[1,128,2048]{2,1,0:T(8,128)(2,1)} %slice.28), channel_id=1, source_target_pairs={{0,6},{1,7},{2,0},{3,1},{4,2},{5,3},{6,4},{7,5},{8,14},{9,15},{10,... | collective-permute-start | bytes 1572872 | tf_op jit(solution)/shard_map/ppermute | solution.py:384
  48.1 4.5 %collective-permute-start = (bf16[2,128,2048]{2,1,0:T(8,128)(2,1)S(1)}, bf16[2,128,2048]{2,1,0:T(8,128)(2,1)}, u32[]{:S(2)}, u32[]{:S(2)}) collective-permute-start(bf16[2,128,2048]{2,1,0:T(8,128)(2,1)S(1)} %normalize.1.refs_0_), channel_id=1, source_target_pairs={{0,1},{1,0},{2,3},{3,2},{4,5},{5,4},{6,7},{7,6},{8,9},{9,8},{10,11... | collective-permute-start | bytes 3145736 | tf_op jit(solution)/shard_map/ppermute | solution.py:418
  52.6 0.0 collective-permute-done.8.refs_2_
  52.6 0.1 collective-permute-start.2
  52.7 0.0 collective-permute-done.9.refs_3_
  52.7 0.4 collective-permute-start.4
  53.1 0.1 copy-done.14
  53.2 2.0 %tile.1 = bf16[8,4,32,256]{3,2,1,0:T(8,128)(2,1)} custom-call(s32[29]{0:T(128)} %stack.89.place_ref, bf16[8,64,128]{2,1,0:T(8,128)(2,1)} %copy-done.6, bf16[8,64,128]{2,1,0:T(8,128)(2,1)} %copy-done.13, bf16[8,64,128]{2,1,0:T(8,128)(2,1)} %copy-done.14, bf16[8,64,128]{2,1,0:T(8,128)(2,1)} %collective-permute-done.9.refs_3_), custom_call_target="tpu_custom_call" | custom-call | tf_op jit(solution)/shard_map/tile/pallas_call | solution.py:96
  55.3 0.0 collective-permute-done.5.refs_6_
  55.3 0.3 collective-permute-done.6.refs_7_
  55.5 5.0 %collective-permute-start.10 = (bf16[1,128,2048]{2,1,0:T(8,128)(2,1)}, bf16[1,128,2048]{2,1,0:T(8,128)(2,1)}, u32[]{:S(2)}, u32[]{:S(2)}) collective-permute-start(bf16[1,128,2048]{2,1,0:T(8,128)(2,1)} %collective-permute-done.5.refs_6_), channel_id=1, source_target_pairs={{0,1},{1,0},{2,3},{3,2},{4,5},{5,4},{6,7},{7,6},{8,9},{9,8},{10,11... | collective-permute-start | bytes 1572872 | tf_op jit(solution)/shard_map/ppermute | solution.py:418
  60.6 0.0 collective-permute-start.11
  60.6 0.0 collective-permute-done.refs_1_
  60.6 0.6 collective-permute-start.19
  61.1 1.3 collective-permute-done.10.refs_8_
  62.4 3.4 %collective-permute-start.20 = (bf16[1024,256]{1,0:T(8,128)(2,1)}, bf16[1024,256]{1,0:T(8,128)(2,1)S(1)}, u32[]{:S(2)}, u32[]{:S(2)}) collective-permute-start(bf16[1024,256]{1,0:T(8,128)(2,1)} %bitcast.25), channel_id=1, source_target_pairs={{0,6},{1,7},{2,0},{3,1},{4,2},{5,3},{6,4},{7,5},{8,14},{9,15},{10,... | collective-permute-start | bytes 1572872 | tf_op jit(solution)/shard_map/ppermute | solution.py:384
  65.8 0.0 collective-permute-done.11.refs_9_
  65.8 0.0 collective-permute-done.2.refs_3_
  65.9 0.0 collective-permute-done.4.refs_5_
  65.9 15.0 %attend.1 = (bf16[2,2,128,128]{3,2,1,0:T(8,128)(2,1)}, bf16[2,2,128,128]{3,2,1,0:T(8,128)(2,1)}, bf16[2,2,128,128]{3,2,1,0:T(8,128)(2,1)}, bf16[2,2,128,128]{3,2,1,0:T(8,128)(2,1)}, bf16[32,32,128]{2,1,0:T(8,128)(2,1)}) custom-call(s32[29]{0:T(128)} %stack.89.place_ref, f32[2]{0:T(128)} %sizes_ref.3, bf16[4,8,64,384]{3,2,1,0:T(8,128)(2,1)} %all-to-all-done.1.source_ref, ...), custom_call_target="tpu_custom_call" | custom-call | flops 5368709120 | bytes 10485760 | tf_op jit(solution)/shard_map/attend/pallas_call | solution.py:214
  80.9 0.0 collective-permute-done.20.refs_10_
  80.9 0.1 collective-permute-start.21
  81.0 0.8 copy-done.5
  81.8 9.2 %all-to-all-start.2 = ((bf16[256,4,128]{2,1,0:T(4,128)(2,1)}), bf16[256,4,128]{2,1,0:T(4,128)(2,1)S(1)}, u32[]{:S(2)}, u32[]{:S(2)}) async-start(bf16[256,4,128]{2,1,0:T(4,128)(2,1)} %bitcast.28), calls=%async_computation.2 | async-start | bytes 524288 | tf_op jit(solution)/shard_map/all_to_all | solution.py:435
  91.0 2.7 %collective-permute-start.12 = (bf16[2,2,128,128]{3,2,1,0:T(8,128)(2,1)}, bf16[2,2,128,128]{3,2,1,0:T(8,128)(2,1)S(1)}, u32[]{:S(2)}, u32[]{:S(2)}) collective-permute-start(bf16[2,2,128,128]{3,2,1,0:T(8,128)(2,1)} %get-tuple-element.20), channel_id=1, source_target_pairs={{0,6},{1,7},{2,0},{3,1},{4,2},{5,3},{6,4},{7,5},{8,14},{9,15},{10,... | collective-permute-start | bytes 393224 | tf_op jit(solution)/shard_map/ppermute | solution.py:384
  93.7 1.7 %collective-permute-start.14 = (bf16[2,2,128,128]{3,2,1,0:T(8,128)(2,1)}, bf16[2,2,128,128]{3,2,1,0:T(8,128)(2,1)S(1)}, u32[]{:S(2)}, u32[]{:S(2)}) collective-permute-start(bf16[2,2,128,128]{3,2,1,0:T(8,128)(2,1)} %get-tuple-element.22), channel_id=1, source_target_pairs={{0,4},{1,5},{2,6},{3,7},{4,0},{5,1},{6,2},{7,3},{8,12},{9,13},{10,... | collective-permute-start | bytes 393224 | tf_op jit(solution)/shard_map/ppermute | solution.py:384
  95.4 1.2 collective-permute-start.23
  96.6 0.7 collective-permute-done.12.refs_1_
  97.3 5.4 %collective-permute-start.15 = (bf16[2,2,128,128]{3,2,1,0:T(8,128)(2,1)}, bf16[2,2,128,128]{3,2,1,0:T(8,128)(2,1)}, u32[]{:S(2)}, u32[]{:S(2)}) collective-permute-start(bf16[2,2,128,128]{3,2,1,0:T(8,128)(2,1)} %get-tuple-element.19.refs_0_), channel_id=1, source_target_pairs={{0,1},{1,0},{2,3},{3,2},{4,5},{5,4},{6,7},{7,6},{8,9},{9,8},{10,11... | collective-permute-start | bytes 393224 | tf_op jit(solution)/shard_map/ppermute | solution.py:418
  102.7 3.2 %collective-permute-start.22 = (bf16[1024,256]{1,0:T(8,128)(2,1)}, bf16[1024,256]{1,0:T(8,128)(2,1)}, u32[]{:S(2)}, u32[]{:S(2)}) collective-permute-start(bf16[1024,256]{1,0:T(8,128)(2,1)} %bitcast.26), channel_id=1, source_target_pairs={{0,1},{1,0},{2,3},{3,2},{4,5},{5,4},{6,7},{7,6},{8,9},{9,8},{10,11... | collective-permute-start | bytes 1572872 | tf_op jit(solution)/shard_map/ppermute | solution.py:418
  105.9 0.1 collective-permute-start.24
  106.0 0.4 collective-permute-start.25
  106.4 0.7 earlier.1
  107.2 8.6 %all-to-all-start.3 = ((bf16[32,32,128]{2,1,0:T(8,128)(2,1)}), bf16[32,32,128]{2,1,0:T(8,128)(2,1)S(1)}, u32[]{:S(2)}, u32[]{:S(2)}) async-start(bf16[32,32,128]{2,1,0:T(8,128)(2,1)} %earlier.1), calls=%async_computation.3 | async-start | bytes 524288 | tf_op jit(solution)/shard_map/all_to_all | solution.py:438
  115.8 0.4 collective-permute-start.16
  116.3 1.0 collective-permute-done.16.refs_5_
  117.3 0.4 collective-permute-start.17
  117.6 1.0 collective-permute-done.17.refs_6_
  118.6 0.4 collective-permute-start.18
  119.0 1.0 collective-permute-done.18.refs_7_
  120.0 0.6 copy-done.12
  120.6 7.1 %all-to-all-done.3.before_ref = bf16[32,32,128]{2,1,0:T(8,128)(2,1)S(1)} async-done(((bf16[32,32,128]{2,1,0:T(8,128)(2,1)}), bf16[32,32,128]{2,1,0:T(8,128)(2,1)S(1)}, u32[]{:S(2)}, u32[]{:S(2)}) %all-to-all-start.3) | async-done | bytes 262176 | tf_op jit(solution)/shard_map/all_to_all | solution.py:438
  127.8 0.6 copy-done.3
  128.4 6.4 %totals.1 = f32[2,128,2048]{2,1,0:T(8,128)} custom-call(s32[29]{0:T(128)} %stack.89.place_ref, f32[2]{0:T(128)} %sizes_ref.3, bf16[32,32,128]{2,1,0:T(8,128)(2,1)} %copy-done.3, bf16[128,2048]{1,0:T(8,128)(2,1)} %initial_ref.1, bf16[2,2,128,128]{3,2,1,0:T(8,128)(2,1)} %get-tuple-element.19.refs_0_, bf16[2,2,128,128]{3,2,1,0:T(8,128)(2,1)} %copy-done.7, ...), custom_call_target="tpu_custom_call" | custom-call | tf_op jit(solution)/shard_map/totals/pallas_call | solution.py:314
  (43 shorter events, 0.2 us)
Async XLA Ops:
  0.0 1.6 %copy-start = (bf16[256,4096]{1,0:T(8,128)(2,1)S(1)}, bf16[256,4096]{1,0:T(8,128)(2,1)}, u32[]{:S(2)}) copy-start(bf16[256,4096]{1,0:T(8,128)(2,1)} %param.15) | copy-start | bytes 6291460
  0.0 2.0 %copy-start.1 = (bf16[2,128,2048]{2,1,0:T(8,128)(2,1)S(1)}, bf16[2,128,2048]{2,1,0:T(8,128)(2,1)}, u32[]{:S(2)}) copy-start(bf16[2,128,2048]{2,1,0:T(8,128)(2,1)} %rows_ref.1) | copy-start | bytes 3145732
  2.8 45.3 %copy-start.2 = (bf16[2,128,2048]{2,1,0:T(8,128)(2,1)}, bf16[2,128,2048]{2,1,0:T(8,128)(2,1)S(1)}, u32[]{:S(2)}) copy-start(bf16[2,128,2048]{2,1,0:T(8,128)(2,1)S(1)} %normalize.1.refs_0_) | copy-start | bytes 3145732
  2.8 39.5 %collective-permute-start.1 = (bf16[2,128,2048]{2,1,0:T(8,128)(2,1)S(1)}, bf16[2,128,2048]{2,1,0:T(8,128)(2,1)}, u32[]{:S(2)}, u32[]{:S(2)}) collective-permute-start(bf16[2,128,2048]{2,1,0:T(8,128)(2,1)S(1)} %normalize.1.refs_0_), channel_id=1, source_target_pairs={{0,2},{1,3},{2,4},{3,5},{4,6},{5,7},{6,0},{7,1},{8,10},{9,11},{10,... | collective-permute-start | bytes 3145736 | tf_op jit(solution)/shard_map/ppermute | solution.py:384
  5.0 38.5 %collective-permute-start.3 = (bf16[2,128,2048]{2,1,0:T(8,128)(2,1)S(1)}, bf16[2,128,2048]{2,1,0:T(8,128)(2,1)}, u32[]{:S(2)}, u32[]{:S(2)}) collective-permute-start(bf16[2,128,2048]{2,1,0:T(8,128)(2,1)S(1)} %normalize.1.refs_0_), channel_id=1, source_target_pairs={{0,6},{1,7},{2,0},{3,1},{4,2},{5,3},{6,4},{7,5},{8,14},{9,15},{10,... | collective-permute-start | bytes 3145736 | tf_op jit(solution)/shard_map/ppermute | solution.py:384
  32.8 5.1 %copy-start.6 = (bf16[8,64,128]{2,1,0:T(8,128)(2,1)}, bf16[8,64,128]{2,1,0:T(8,128)(2,1)S(1)}, u32[]{:S(2)}) copy-start(bf16[8,64,128]{2,1,0:T(8,128)(2,1)S(1)} %slice.29.refs_0_) | copy-start | bytes 393220
  32.9 15.2 %collective-permute-start.7 = (bf16[8,64,128]{2,1,0:T(8,128)(2,1)S(1)}, bf16[8,64,128]{2,1,0:T(8,128)(2,1)S(1)}, u32[]{:S(2)}, u32[]{:S(2)}) collective-permute-start(bf16[8,64,128]{2,1,0:T(8,128)(2,1)S(1)} %slice.29.refs_0_), channel_id=1, source_target_pairs={{0,24},{8,0},{16,8},{24,16},{32,56},{40,32},{48,40},{56,48},{64,88... | collective-permute-start | bytes 393224 | tf_op jit(solution)/shard_map/ppermute | solution.py:344
  35.4 17.2 %collective-permute-start.8 = (bf16[8,64,128]{2,1,0:T(8,128)(2,1)S(1)}, bf16[8,64,128]{2,1,0:T(8,128)(2,1)S(1)}, u32[]{:S(2)}, u32[]{:S(2)}) collective-permute-start(bf16[8,64,128]{2,1,0:T(8,128)(2,1)S(1)} %slice.29.refs_0_), channel_id=1, source_target_pairs={{0,16},{8,24},{16,0},{24,8},{32,48},{40,56},{48,32},{56,40},{64,80... | collective-permute-start | bytes 393224 | tf_op jit(solution)/shard_map/ppermute | solution.py:344
  35.9 16.8 %collective-permute-start.9 = (bf16[8,64,128]{2,1,0:T(8,128)(2,1)S(1)}, bf16[8,64,128]{2,1,0:T(8,128)(2,1)}, u32[]{:S(2)}, u32[]{:S(2)}) collective-permute-start(bf16[8,64,128]{2,1,0:T(8,128)(2,1)S(1)} %slice.29.refs_0_), channel_id=1, source_target_pairs={{0,8},{8,16},{16,24},{24,0},{32,40},{40,48},{48,56},{56,32},{64,72... | collective-permute-start | bytes 393224 | tf_op jit(solution)/shard_map/ppermute | solution.py:344
  38.0 27.9 %all-to-all-start.1 = ((bf16[4,8,64,384]{3,2,1,0:T(8,128)(2,1)}), bf16[4,8,64,384]{3,2,1,0:T(8,128)(2,1)}, u32[]{:S(2)}, u32[]{:S(2)}) async-start(bf16[4,8,64,384]{3,2,1,0:T(8,128)(2,1)} %broadcast_in_dim.2), calls=%async_computation.1 | async-start | bytes 3145728 | tf_op jit(solution)/shard_map/all_to_all | solution.py:353
  43.4 11.8 %collective-permute-start.5 = (bf16[1,128,2048]{2,1,0:T(8,128)(2,1)S(1)}, bf16[1,128,2048]{2,1,0:T(8,128)(2,1)}, u32[]{:S(2)}, u32[]{:S(2)}) collective-permute-start(bf16[1,128,2048]{2,1,0:T(8,128)(2,1)S(1)} %slice.27), channel_id=1, source_target_pairs={{0,2},{1,3},{2,4},{3,5},{4,6},{5,7},{6,0},{7,1},{8,10},{9,11},{10,... | collective-permute-start | bytes 1572872 | tf_op jit(solution)/shard_map/ppermute | solution.py:384
  45.4 10.1 %collective-permute-start.6 = (bf16[1,128,2048]{2,1,0:T(8,128)(2,1)}, bf16[1,128,2048]{2,1,0:T(8,128)(2,1)}, u32[]{:S(2)}, u32[]{:S(2)}) collective-permute-start(bf16[1,128,2048]{2,1,0:T(8,128)(2,1)} %slice.28), channel_id=1, source_target_pairs={{0,6},{1,7},{2,0},{3,1},{4,2},{5,3},{6,4},{7,5},{8,14},{9,15},{10,... | collective-permute-start | bytes 1572872 | tf_op jit(solution)/shard_map/ppermute | solution.py:384
  48.1 5.0 %copy-start.13 = (bf16[8,64,128]{2,1,0:T(8,128)(2,1)}, bf16[8,64,128]{2,1,0:T(8,128)(2,1)S(1)}, u32[]{:S(2)}) copy-start(bf16[8,64,128]{2,1,0:T(8,128)(2,1)S(1)} %collective-permute-done.7.refs_1_) | copy-start | bytes 393220
  48.1 12.5 %collective-permute-start = (bf16[2,128,2048]{2,1,0:T(8,128)(2,1)S(1)}, bf16[2,128,2048]{2,1,0:T(8,128)(2,1)}, u32[]{:S(2)}, u32[]{:S(2)}) collective-permute-start(bf16[2,128,2048]{2,1,0:T(8,128)(2,1)S(1)} %normalize.1.refs_0_), channel_id=1, source_target_pairs={{0,1},{1,0},{2,3},{3,2},{4,5},{5,4},{6,7},{7,6},{8,9},{9,8},{10,11... | collective-permute-start | bytes 3145736 | tf_op jit(solution)/shard_map/ppermute | solution.py:418
  52.6 0.7 copy-start.14
  52.6 13.3 %collective-permute-start.2 = (bf16[2,128,2048]{2,1,0:T(8,128)(2,1)}, bf16[2,128,2048]{2,1,0:T(8,128)(2,1)}, u32[]{:S(2)}, u32[]{:S(2)}) collective-permute-start(bf16[2,128,2048]{2,1,0:T(8,128)(2,1)} %collective-permute-done.1.refs_2_), channel_id=1, source_target_pairs={{0,1},{1,0},{2,3},{3,2},{4,5},{5,4},{6,7},{7,6},{8,9},{9,8},{10,11... | collective-permute-start | bytes 3145736 | tf_op jit(solution)/shard_map/ppermute | solution.py:418
  52.7 13.2 %collective-permute-start.4 = (bf16[2,128,2048]{2,1,0:T(8,128)(2,1)}, bf16[2,128,2048]{2,1,0:T(8,128)(2,1)}, u32[]{:S(2)}, u32[]{:S(2)}) collective-permute-start(bf16[2,128,2048]{2,1,0:T(8,128)(2,1)} %collective-permute-done.3.refs_4_), channel_id=1, source_target_pairs={{0,1},{1,0},{2,3},{3,2},{4,5},{5,4},{6,7},{7,6},{8,9},{9,8},{10,11... | collective-permute-start | bytes 3145736 | tf_op jit(solution)/shard_map/ppermute | solution.py:418
  55.5 6.9 %collective-permute-start.10 = (bf16[1,128,2048]{2,1,0:T(8,128)(2,1)}, bf16[1,128,2048]{2,1,0:T(8,128)(2,1)}, u32[]{:S(2)}, u32[]{:S(2)}) collective-permute-start(bf16[1,128,2048]{2,1,0:T(8,128)(2,1)} %collective-permute-done.5.refs_6_), channel_id=1, source_target_pairs={{0,1},{1,0},{2,3},{3,2},{4,5},{5,4},{6,7},{7,6},{8,9},{9,8},{10,11... | collective-permute-start | bytes 1572872 | tf_op jit(solution)/shard_map/ppermute | solution.py:418
  60.6 5.3 %collective-permute-start.11 = (bf16[1,128,2048]{2,1,0:T(8,128)(2,1)}, bf16[1,128,2048]{2,1,0:T(8,128)(2,1)}, u32[]{:S(2)}, u32[]{:S(2)}) collective-permute-start(bf16[1,128,2048]{2,1,0:T(8,128)(2,1)} %collective-permute-done.6.refs_7_), channel_id=1, source_target_pairs={{0,1},{1,0},{2,3},{3,2},{4,5},{5,4},{6,7},{7,6},{8,9},{9,8},{10,11... | collective-permute-start | bytes 1572872 | tf_op jit(solution)/shard_map/ppermute | solution.py:418
  60.6 20.3 %collective-permute-start.19 = (bf16[1024,256]{1,0:T(8,128)(2,1)}, bf16[1024,256]{1,0:T(8,128)(2,1)S(1)}, u32[]{:S(2)}, u32[]{:S(2)}) collective-permute-start(bf16[1024,256]{1,0:T(8,128)(2,1)} %bitcast.24), channel_id=1, source_target_pairs={{0,2},{1,3},{2,4},{3,5},{4,6},{5,7},{6,0},{7,1},{8,10},{9,11},{10,... | collective-permute-start | bytes 1572872 | tf_op jit(solution)/shard_map/ppermute | solution.py:384
  62.4 18.5 %collective-permute-start.20 = (bf16[1024,256]{1,0:T(8,128)(2,1)}, bf16[1024,256]{1,0:T(8,128)(2,1)S(1)}, u32[]{:S(2)}, u32[]{:S(2)}) collective-permute-start(bf16[1024,256]{1,0:T(8,128)(2,1)} %bitcast.25), channel_id=1, source_target_pairs={{0,6},{1,7},{2,0},{3,1},{4,2},{5,3},{6,4},{7,5},{8,14},{9,15},{10,... | collective-permute-start | bytes 1572872 | tf_op jit(solution)/shard_map/ppermute | solution.py:384
  80.9 46.8 %copy-start.4 = (bf16[1024,256]{1,0:T(8,128)(2,1)}, bf16[1024,256]{1,0:T(8,128)(2,1)S(1)}, u32[]{:S(2)}) copy-start(bf16[1024,256]{1,0:T(8,128)(2,1)S(1)} %collective-permute-done.19.refs_9_) | copy-start | bytes 1572868
  80.9 0.9 copy-start.5
  80.9 25.1 %collective-permute-start.21 = (bf16[1024,256]{1,0:T(8,128)(2,1)S(1)}, bf16[1024,256]{1,0:T(8,128)(2,1)}, u32[]{:S(2)}, u32[]{:S(2)}) collective-permute-start(bf16[1024,256]{1,0:T(8,128)(2,1)S(1)} %collective-permute-done.19.refs_9_), channel_id=1, source_target_pairs={{0,2},{1,3},{2,4},{3,5},{4,6},{5,7},{6,0},{7,1},{8,10},{9,11},{10,... | collective-permute-start | bytes 1572872 | tf_op jit(solution)/shard_map/ppermute | solution.py:384
  81.8 24.6 %all-to-all-start.2 = ((bf16[256,4,128]{2,1,0:T(4,128)(2,1)}), bf16[256,4,128]{2,1,0:T(4,128)(2,1)S(1)}, u32[]{:S(2)}, u32[]{:S(2)}) async-start(bf16[256,4,128]{2,1,0:T(4,128)(2,1)} %bitcast.28), calls=%async_computation.2 | async-start | bytes 524288 | tf_op jit(solution)/shard_map/all_to_all | solution.py:435
  91.0 6.3 %collective-permute-start.12 = (bf16[2,2,128,128]{3,2,1,0:T(8,128)(2,1)}, bf16[2,2,128,128]{3,2,1,0:T(8,128)(2,1)S(1)}, u32[]{:S(2)}, u32[]{:S(2)}) collective-permute-start(bf16[2,2,128,128]{3,2,1,0:T(8,128)(2,1)} %get-tuple-element.20), channel_id=1, source_target_pairs={{0,6},{1,7},{2,0},{3,1},{4,2},{5,3},{6,4},{7,5},{8,14},{9,15},{10,... | collective-permute-start | bytes 393224 | tf_op jit(solution)/shard_map/ppermute | solution.py:384
  93.7 9.0 %collective-permute-start.13 = (bf16[2,2,128,128]{3,2,1,0:T(8,128)(2,1)}, bf16[2,2,128,128]{3,2,1,0:T(8,128)(2,1)S(1)}, u32[]{:S(2)}, u32[]{:S(2)}) collective-permute-start(bf16[2,2,128,128]{3,2,1,0:T(8,128)(2,1)} %get-tuple-element.21), channel_id=1, source_target_pairs={{0,2},{1,3},{2,4},{3,5},{4,6},{5,7},{6,0},{7,1},{8,10},{9,11},{10,... | collective-permute-start | bytes 393224 | tf_op jit(solution)/shard_map/ppermute | solution.py:384
  93.7 12.2 %collective-permute-start.14 = (bf16[2,2,128,128]{3,2,1,0:T(8,128)(2,1)}, bf16[2,2,128,128]{3,2,1,0:T(8,128)(2,1)S(1)}, u32[]{:S(2)}, u32[]{:S(2)}) collective-permute-start(bf16[2,2,128,128]{3,2,1,0:T(8,128)(2,1)} %get-tuple-element.22), channel_id=1, source_target_pairs={{0,4},{1,5},{2,6},{3,7},{4,0},{5,1},{6,2},{7,3},{8,12},{9,13},{10,... | collective-permute-start | bytes 393224 | tf_op jit(solution)/shard_map/ppermute | solution.py:384
  95.4 24.6 %collective-permute-start.23 = (bf16[1024,256]{1,0:T(8,128)(2,1)S(1)}, bf16[1024,256]{1,0:T(8,128)(2,1)}, u32[]{:S(2)}, u32[]{:S(2)}) collective-permute-start(bf16[1024,256]{1,0:T(8,128)(2,1)S(1)} %collective-permute-done.19.refs_9_), channel_id=1, source_target_pairs={{0,1},{1,0},{2,3},{3,2},{4,5},{5,4},{6,7},{7,6},{8,9},{9,8},{10,11... | collective-permute-start | bytes 1572872 | tf_op jit(solution)/shard_map/ppermute | solution.py:418
  97.3 30.4 %copy-start.7 = (bf16[2,2,128,128]{3,2,1,0:T(8,128)(2,1)}, bf16[2,2,128,128]{3,2,1,0:T(8,128)(2,1)S(1)}, u32[]{:S(2)}) copy-start(bf16[2,2,128,128]{3,2,1,0:T(8,128)(2,1)S(1)} %collective-permute-done.12.refs_1_) | copy-start | bytes 393220
  97.3 18.5 %collective-permute-start.15 = (bf16[2,2,128,128]{3,2,1,0:T(8,128)(2,1)}, bf16[2,2,128,128]{3,2,1,0:T(8,128)(2,1)}, u32[]{:S(2)}, u32[]{:S(2)}) collective-permute-start(bf16[2,2,128,128]{3,2,1,0:T(8,128)(2,1)} %get-tuple-element.19.refs_0_), channel_id=1, source_target_pairs={{0,1},{1,0},{2,3},{3,2},{4,5},{5,4},{6,7},{7,6},{8,9},{9,8},{10,11... | collective-permute-start | bytes 393224 | tf_op jit(solution)/shard_map/ppermute | solution.py:418
  102.7 25.1 %copy-start.8 = (bf16[2,2,128,128]{3,2,1,0:T(8,128)(2,1)}, bf16[2,2,128,128]{3,2,1,0:T(8,128)(2,1)S(1)}, u32[]{:S(2)}) copy-start(bf16[2,2,128,128]{3,2,1,0:T(8,128)(2,1)S(1)} %collective-permute-done.13.refs_2_) | copy-start | bytes 393220
  102.7 17.3 %collective-permute-start.22 = (bf16[1024,256]{1,0:T(8,128)(2,1)}, bf16[1024,256]{1,0:T(8,128)(2,1)}, u32[]{:S(2)}, u32[]{:S(2)}) collective-permute-start(bf16[1024,256]{1,0:T(8,128)(2,1)} %bitcast.26), channel_id=1, source_target_pairs={{0,1},{1,0},{2,3},{3,2},{4,5},{5,4},{6,7},{7,6},{8,9},{9,8},{10,11... | collective-permute-start | bytes 1572872 | tf_op jit(solution)/shard_map/ppermute | solution.py:418
  105.9 21.9 %copy-start.9 = (bf16[2,2,128,128]{3,2,1,0:T(8,128)(2,1)}, bf16[2,2,128,128]{3,2,1,0:T(8,128)(2,1)S(1)}, u32[]{:S(2)}) copy-start(bf16[2,2,128,128]{3,2,1,0:T(8,128)(2,1)S(1)} %collective-permute-done.14.refs_3_) | copy-start | bytes 393220
  105.9 14.7 %collective-permute-start.24 = (bf16[1024,256]{1,0:T(8,128)(2,1)}, bf16[1024,256]{1,0:T(8,128)(2,1)}, u32[]{:S(2)}, u32[]{:S(2)}) collective-permute-start(bf16[1024,256]{1,0:T(8,128)(2,1)} %copy-done.5), channel_id=1, source_target_pairs={{0,1},{1,0},{2,3},{3,2},{4,5},{5,4},{6,7},{7,6},{8,9},{9,8},{10,11... | collective-permute-start | bytes 1572872 | tf_op jit(solution)/shard_map/ppermute | solution.py:418
  106.0 21.7 %collective-permute-start.25 = (bf16[1024,256]{1,0:T(8,128)(2,1)}, bf16[1024,256]{1,0:T(8,128)(2,1)}, u32[]{:S(2)}, u32[]{:S(2)}) collective-permute-start(bf16[1024,256]{1,0:T(8,128)(2,1)} %collective-permute-done.21.refs_11_), channel_id=1, source_target_pairs={{0,1},{1,0},{2,3},{3,2},{4,5},{5,4},{6,7},{7,6},{8,9},{9,8},{10,11... | collective-permute-start | bytes 1572872 | tf_op jit(solution)/shard_map/ppermute | solution.py:418
  107.2 20.6 %all-to-all-start.3 = ((bf16[32,32,128]{2,1,0:T(8,128)(2,1)}), bf16[32,32,128]{2,1,0:T(8,128)(2,1)S(1)}, u32[]{:S(2)}, u32[]{:S(2)}) async-start(bf16[32,32,128]{2,1,0:T(8,128)(2,1)} %earlier.1), calls=%async_computation.3 | async-start | bytes 524288 | tf_op jit(solution)/shard_map/all_to_all | solution.py:438
  115.8 1.4 %collective-permute-start.16 = (bf16[2,2,128,128]{3,2,1,0:T(8,128)(2,1)S(1)}, bf16[2,2,128,128]{3,2,1,0:T(8,128)(2,1)S(1)}, u32[]{:S(2)}, u32[]{:S(2)}) collective-permute-start(bf16[2,2,128,128]{3,2,1,0:T(8,128)(2,1)S(1)} %collective-permute-done.12.refs_1_), channel_id=1, source_target_pairs={{0,1},{1,0},{2,3},{3,2},{4,5},{5,4},{6,7},{7,6},{8,9},{9,8},{10,11... | collective-permute-start | bytes 393224 | tf_op jit(solution)/shard_map/ppermute | solution.py:418
  117.3 10.5 %copy-start.10 = (bf16[2,2,128,128]{3,2,1,0:T(8,128)(2,1)}, bf16[2,2,128,128]{3,2,1,0:T(8,128)(2,1)S(1)}, u32[]{:S(2)}) copy-start(bf16[2,2,128,128]{3,2,1,0:T(8,128)(2,1)S(1)} %collective-permute-done.16.refs_5_) | copy-start | bytes 393220
  117.3 1.3 collective-permute-start.17
  118.6 9.2 %copy-start.11 = (bf16[2,2,128,128]{3,2,1,0:T(8,128)(2,1)}, bf16[2,2,128,128]{3,2,1,0:T(8,128)(2,1)S(1)}, u32[]{:S(2)}) copy-start(bf16[2,2,128,128]{3,2,1,0:T(8,128)(2,1)S(1)} %collective-permute-done.17.refs_6_) | copy-start | bytes 393220
  118.6 1.3 collective-permute-start.18
  120.0 0.6 copy-start.12
  127.8 0.7 copy-start.3
